TPU v7x, 256 devices: a whole 4x4x8 slice. The times are simulated.
256 devices in a mesh: rep: 8 (over y, core), shard: 32 (over x, z).
Axes of the slice: x: 4, y: 4, z: 8, core: 2. Of those that a mesh axis runs over, the one named last changes fastest.
Arguments:
- grad_out: bfloat16 [8, 4096, 8192], P('rep', 'shard'), may hold values from -6 to 6
- error_out: bfloat16 [8, 4096, 8192], P('rep', 'shard'), may hold values from -4 to 4
- basis_out: float32 [8192, 32], replicated, may hold values from -0.0625 to 0.0625
- overflow: int32 [8], P('rep'), may hold values from 0 to 1, as said below
Outputs:
- update_out: bfloat16 [4096, 8192], P('shard')
- new_error_out: bfloat16 [8, 4096, 8192], P('rep', 'shard')
- new_basis_out: float32 [8192, 32], replicated
Inputs may be any that keep to these rules, and one draw needn't show every extreme that they name: `overflow`: at least one replica's flag is 1, at least one is 0, and at most half of the 8 replicas have flag 1.
All inputs are finite; a program needn't handle non-finite values.
Results may differ from a plain program's by a relative error of at most 0.002.
Values sent between devices are 32-bit elements; how exact they have to be, the bound alone decides.
A program may use at most 64 MiB of HBM per device.

v0:
```python
import jax
import jax.numpy as jnp
from jax import lax
from jax.sharding import PartitionSpec as P


def project(matrix, basis):
    return jnp.dot(matrix, basis, precision=lax.Precision.HIGHEST)


def transpose_project(matrix, ortho):
    return jnp.einsum("kc,kj->cj", matrix, ortho, precision=lax.Precision.HIGHEST)


def orthonormal(left):
    gram = lax.psum(jnp.dot(left.T, left, precision=lax.Precision.HIGHEST), "shard")
    rank_size = gram.shape[0]
    shifted = gram + 1e-05 * (jnp.trace(gram) / rank_size) * jnp.eye(rank_size, dtype=jnp.float32)
    lower = jnp.linalg.cholesky(shifted)
    return jax.scipy.linalg.solve_triangular(lower, left.T, lower=True).T


def on_device(grad_out, error_out, basis_out, overflow):
    healthy = 1.0 - overflow.astype(jnp.float32)
    weight = healthy[0]
    corrected = grad_out[0].astype(jnp.float32) + error_out[0].astype(jnp.float32)
    left, kept_total = lax.psum((weight * project(corrected, basis_out), healthy), "rep")
    ortho = orthonormal(left / kept_total[0])
    new_basis_out = lax.psum(weight * transpose_project(corrected, ortho), ("rep", "shard"))
    new_basis_out = new_basis_out / kept_total[0]
    approx = jnp.einsum("kj,cj->kc", ortho, new_basis_out, precision=lax.Precision.HIGHEST)
    update_out = approx.astype(jnp.bfloat16)
    new_error_out = jnp.where(
        weight > 0.5, corrected - approx, error_out[0].astype(jnp.float32)
    ).astype(jnp.bfloat16)[None]
    return (update_out, new_error_out, new_basis_out)


def solution(mesh):
    return jax.shard_map(
        on_device,
        mesh=mesh,
        in_specs=(P("rep", "shard", None), P("rep", "shard", None), P(), P("rep")),
        out_specs=(P("shard", None), P("rep", "shard", None), P()),
        check_vma=False,
    )
```

profile of v0, /device:TPU:1, one launch (start us, length us, event | category | flops | bytes accessed | tf_op | source)
XLA Modules:
  0.0 463.4 jit_solution(2255661696388770675)
XLA Ops:
  7.2 0.0 copy-start
  7.2 0.0 all-reduce.3.cloned.1.call-start
  8.0 0.5 copy-done
  8.4 0.0 copy-start.1
  8.4 5.9 %fusion.7 = f32[128,32]{0,1:T(8,128)S(1)} fusion(f32[8192,32]{0,1:T(8,128)S(1)} %copy-done, bf16[1,128,8192]{2,1,0:T(8,128)(2,1)} %param.4, bf16[1,128,8192]{2,1,0:T(8,128)(2,1)} %param.5, f32[]{:T(128)} %bitcast), kind=kOutput, calls=%fused_computation.10 | convolution fusion | flops 405803008 | bytes 5259268 | tf_op jit(solution)/shard_map/dot_general | solution.py:8
  14.3 25.5 %all-reduce = (f32[128,32]{0,1:T(8,128)S(1)}, f32[]{:T(128)}) all-reduce(f32[128,32]{0,1:T(8,128)S(1)} %fusion.7, f32[]{:T(128)} %bitcast), channel_id=1, replica_groups=mesh['rep'=8,'shard'=32] {'rep'}, use_global_device_ids=true, to_apply=%region_0.0 | all-reduce | flops 4097 | bytes 32776 | tf_op jit(solution)/shard_map/psum | solution.py:27
  39.8 0.8 fusion.12
  40.6 118.1 %psum.30 = f32[32,32]{1,0:T(8,128)S(1)} all-reduce(f32[32,32]{1,0:T(8,128)S(1)} %fusion.12), channel_id=1, replica_groups=mesh['rep'=8,'shard'=32] {'shard'}, use_global_device_ids=true, to_apply=%region_2.0 | all-reduce | flops 1024 | bytes 8192 | tf_op jit(solution)/shard_map/psum | solution.py:16
  158.7 0.6 select_reduce_fusion.1
  159.9 0.1 copy.7
  160.0 2.9 cholesky.17
  163.0 0.6 compare_reduce_fusion
  163.6 0.7 fusion.8
  164.3 2.4 custom-call.7
  166.7 0.9 fusion.9
  167.6 0.0 copy-done.1
  167.6 5.3 %convolution_multiply_fusion = f32[8192,32]{0,1:T(8,128)} fusion(f32[32,128]{1,0:T(8,128)S(1)} %fusion.9, bf16[1,128,8192]{2,1,0:T(8,128)(2,1)S(1)} %copy-done.1, bf16[1,128,8192]{2,1,0:T(8,128)(2,1)} %param.5, f32[]{:T(128)} %bitcast), kind=kOutput, calls=%fused_computation | convolution fusion | flops 406061056 | bytes 5259268 | tf_op jit(solution)/shard_map/kc,kj->cj/dot_general | solution.py:12
  172.9 0.0 all-reduce.3.cloned.1.call-update
  172.9 275.8 %all-reduce.3.cloned.1.call-done = f32[8192,32]{0,1:T(8,128)} async-done(((f32[8192,32]{0,1:T(8,128)}), f32[8192,32]{0,1:T(8,128)}) %all-reduce.3.cloned.1.call-update) | async-done | bytes 1048592 | tf_op jit(solution)/shard_map/psum | solution.py:29
  448.8 0.0 copy-start.2
  448.8 2.1 broadcast_divide_fusion
  450.9 0.0 copy-done.2
  450.9 0.0 copy-start.3
  450.9 5.7 %fusion.2 = (bf16[1,128,8192]{2,1,0:T(8,128)(2,1)}, bf16[128,8192]{1,0:T(8,128)(2,1)}) fusion(bf16[1,128,8192]{2,1,0:T(8,128)(2,1)S(1)} %copy-done.1, bf16[1,128,8192]{2,1,0:T(8,128)(2,1)S(1)} %copy-done.2, pred[]{:T(512)S(6)} %gt.3, f32[32,128]{1,0:T(8,128)S(1)} %fusion.9, f32[8192,32]{0,1:T(8,128)S(1)} %broadcast_divide_fusion), kind=kOutput, calls=%fused_computation.5 | convolution fusion | flops 409993216 | bytes 9453569 | tf_op jit(solution)/shard_map/kj,cj->kc/dot_general | solution.py:31
  456.5 0.0 copy-done.3
  (3 shorter events, 0.1 us)
Async XLA Ops:
  7.2 1.2 copy-start
  7.2 441.6 %all-reduce.3.cloned.1.call-start = ((), (), s32[]{:S(2)}) async-start(), calls=%async_computation | async-start | bytes 2097152 | tf_op jit(solution)/shard_map/psum | solution.py:29
  8.4 159.2 %copy-start.1 = (bf16[1,128,8192]{2,1,0:T(8,128)(2,1)S(1)}, bf16[1,128,8192]{2,1,0:T(8,128)(2,1)}, u32[]{:S(2)}) copy-start(bf16[1,128,8192]{2,1,0:T(8,128)(2,1)} %param.4) | copy-start | bytes 6291460
  448.8 2.1 copy-start.2
  450.9 5.7 %copy-start.3 = (f32[8192,32]{0,1:T(8,128)}, f32[8192,32]{0,1:T(8,128)S(1)}, u32[]{:S(2)}) copy-start(f32[8192,32]{0,1:T(8,128)S(1)} %broadcast_divide_fusion) | copy-start | bytes 3145732
Sparse Core Ops, SparseCore 0:
  173.1 275.6 all-reduce.2
where the time goes:
time: 464 us; the launch traced here: 463 us
  waiting for transfers between devices  276 us (59%)
  blocking collectives  144 us (31%)
  matrix products  18.5 us (4%)
  between operations  15.5 us (3%)
  other arithmetic  9.39 us (2%)
    psum x1, waiting for transfers between devices, on_device(): lax.psum(weight * transpose_project(corrected, ortho), ('rep', 'shard'))  276 us
    psum x1, blocking collectives, orthonormal(): lax.psum(jnp.dot(left.T, left, precision=lax.Precision.HIGHEST), 'shard')  118 us
    psum x1, blocking collectives, on_device(): lax.psum((weight * project(corrected, basis_out), healthy), 'rep')  25.5 us
  transfers between devices with their start and end apart: 1, of which 1 were waited for; matrix products, arithmetic and copies ran while one was open for 0% of the time, Pallas kernels for 0%

commit v1 on v0

v1 whole, which is shorter than its diff:
```python
import functools

import jax
import jax.numpy as jnp
from jax import lax
from jax.experimental import pallas as pl
from jax.experimental.pallas import tpu as pltpu
from jax.sharding import PartitionSpec as P

MESH = pl.DeviceIdType.MESH
F32, BF16 = jnp.float32, jnp.bfloat16
D, RANK, ROWS = 8192, 32, 128
CHUNKS = 4
CHUNK = D // CHUNKS
NY, NX, NZ = 4, 4, 8


def pieces(value):
    first = value.astype(BF16)
    rest = value - first.astype(F32)
    second = rest.astype(BF16)
    third = (rest - second.astype(F32)).astype(BF16)
    return first, second, third


def full_dot(a, b, dims):
    return lax.dot_general(a, b, (dims, ((), ())), precision=lax.Precision.HIGHEST, preferred_element_type=F32)


def inverse_factor(gram):
    row = lax.broadcasted_iota(jnp.int32, (RANK, 128), 0)
    lane = lax.broadcasted_iota(jnp.int32, (RANK, 128), 1)
    diagonal = row == lane
    trace = jnp.sum(jnp.where(diagonal, gram, 0.0), axis=(0, 1), keepdims=True)
    shift = 1e-05 * (trace / RANK)
    work = jnp.where(lane < RANK, gram, 0.0) + jnp.where(diagonal, shift, 0.0)
    work = work + jnp.where(lane - RANK == row, 1.0, 0.0)
    for j in range(RANK - 1):
        column = jnp.broadcast_to(work[:, j : j + 1], (RANK, 128))
        scaled = work[j : j + 1, :] / column[j : j + 1, :]
        work = work - jnp.where(row > j, column, 0.0) * scaled
    pivots = jnp.sum(jnp.where(diagonal, work, 0.0), axis=1, keepdims=True)
    inverse = work * lax.rsqrt(pivots)
    return pltpu.roll(inverse, 128 - RANK, 1)


def reduce_kernel(
    grad_hbm, error_hbm, basis_hbm, overflow, nb_out, ortho_out,
    ge, bt, lc, ly, gx, gz, sp, rc, t1, r1, t2, r2, zb, nb, ov,
    in_sem, lc_s, lc_r, ly_s, ly_r, gx_s, gx_r, gz_s, gz_r, rc_s, rc_r,
    p1_s, p1_r, p2_s, p2_r, z_s, z_r, a2_s, a2_r, a1_s, a1_r, ac_s, ac_r, out_sem,
):
    rep, shard = lax.axis_index("rep"), lax.axis_index("shard")
    y, c = rep // 2, rep % 2
    x, z = shard // NZ, shard % NZ

    def at(y_, c_, x_, z_):
        return (y_ * 2 + c_, x_ * NZ + z_)

    partner = at(y, 1 - c, x, z)

    def along_y(d):
        return at((y + d) % NY, c, x, z)

    def along_x(d):
        return at(y, c, (x + d) % NX, z)

    def along_z(d):
        return at(y, c, x, (z + d) % NZ)

    def remote(src, dst, send, recv, device):
        return pltpu.make_async_remote_copy(
            src_ref=src, dst_ref=dst, send_sem=send, recv_sem=recv, device_id=device, device_id_type=MESH
        )

    sent = []

    def send(src, dst, send_sem, recv_sem, device):
        copy = remote(src, dst, send_sem, recv_sem, device)
        copy.start()
        sent.append(copy)

    def arrived(dst, recv_sem):
        remote(dst, dst, lc_s.at[0], recv_sem, partner).wait_recv()

    loads = []
    for k in range(CHUNKS):
        cols = pl.ds(k * CHUNK, CHUNK)
        group = [
            pltpu.make_async_copy(basis_hbm.at[:, cols], bt.at[:, cols], in_sem.at[0, k]),
            pltpu.make_async_copy(grad_hbm.at[:, cols], ge.at[pl.ds(0, ROWS), cols], in_sem.at[1, k]),
            pltpu.make_async_copy(error_hbm.at[:, cols], ge.at[pl.ds(ROWS, ROWS), cols], in_sem.at[2, k]),
        ]
        for copy in group:
            copy.start()
        loads.append(group)

    barrier = pltpu.get_barrier_semaphore()
    others = [partner]
    others += [along_y(d) for d in range(1, NY)] + [along_x(d) for d in range(1, NX)]
    others += [along_z(d) for d in range(1, NZ)]
    for other in others:
        pl.semaphore_signal(barrier, inc=1, device_id=other, device_id_type=MESH)

    health = jnp.full((8, 128), 1.0 - overflow[0].astype(F32), F32)
    acc = jnp.zeros((3 * RANK, 2 * ROWS), F32)
    for k in range(CHUNKS):
        for copy in loads[k]:
            copy.wait()
        cols = pl.ds(k * CHUNK, CHUNK)
        basis = jnp.concatenate(pieces(bt[:, cols]), axis=0)
        acc += lax.dot_general(basis, ge[:, cols], (((1,), (1,)), ((), ())), preferred_element_type=F32)
    both = acc[:RANK] + acc[RANK : 2 * RANK] + acc[2 * RANK :]
    lc[0, :RANK] = (both[:, :ROWS] + both[:, ROWS:]) * health[:1]
    lc[0, RANK:] = health

    pl.semaphore_wait(barrier, len(others))

    send(lc.at[0], lc.at[1], lc_s.at[0], lc_r.at[0], partner)
    arrived(lc.at[1], lc_r.at[0])
    ly[y] = lc[0] + lc[1]
    for d in range(1, NY):
        send(ly.at[y], ly.at[y], ly_s.at[d], ly_r.at[y], along_y(d))
    for d in range(1, NY):
        source = (y + d) % NY
        arrived(ly.at[source], ly_r.at[source])
    total = ly[0] + ly[1] + ly[2] + ly[3]
    kept = total[RANK : RANK + 1]
    left = total[:RANK] / kept

    gram = full_dot(left, jnp.concatenate([left] * 4, axis=0), ((1,), (1,)))
    lane_group = lax.broadcasted_iota(jnp.int32, (8, 128), 1) // RANK
    packed = gram[:8]
    for b in range(1, 4):
        packed = jnp.where(lane_group == b, gram[8 * b : 8 * b + 8], packed)
    gx[x] = packed
    for d in range(1, NX):
        send(gx.at[x], gx.at[x], gx_s.at[d], gx_r.at[x], along_x(d))

    weighted = jnp.concatenate(pieces(left * (health[:1] / kept)), axis=0)
    weighted = jnp.concatenate([weighted, weighted], axis=1)

    def product(block):
        cols = pl.ds(pl.multiple_of(block * 128, 512), 512)
        out = lax.dot_general(weighted, ge[:, cols], (((1,), (0,)), ((), ())), preferred_element_type=F32)
        return out[:RANK] + out[RANK : 2 * RANK] + out[2 * RANK :]

    first = (x, y)
    second = (y, x)
    along_first = (along_x, along_y)
    along_second = (along_y, along_x)
    order = [(d, h) for d in (1, 2, 3, 0) for h in range(2)]
    for i, (d, h) in enumerate(order):
        group = h * 16 + ((first[h] + d) % 4) * 4
        theirs = (1 - c) * 32 + group
        value = product(theirs)
        for q in range(4):
            sp[group + q] = value[:, q * 128 : (q + 1) * 128]
        send(sp.at[pl.ds(group, 4)], rc.at[pl.ds(group, 4)], rc_s.at[i], rc_r.at[i], partner)
    for i, (d, h) in enumerate(order):
        p = (first[h] + d) % 4
        group = h * 16 + p * 4
        value = product(c * 32 + group)
        arrived(rc.at[pl.ds(group, 4)], rc_r.at[i])
        if d == 0:
            for q in range(4):
                r1[h, p, q] = value[:, q * 128 : (q + 1) * 128] + rc[group + q]
        else:
            for q in range(4):
                t1[group + q] = value[:, q * 128 : (q + 1) * 128] + rc[group + q]
            send(t1.at[pl.ds(group, 4)], r1.at[h, first[h]], p1_s.at[h, d], p1_r.at[h, first[h]], along_first[h](d))

    for d in range(1, NX):
        source = (x + d) % NX
        arrived(gx.at[source], gx_r.at[source])
    gz[z] = gx[0] + gx[1] + gx[2] + gx[3]
    for d in range(1, NZ):
        send(gz.at[z], gz.at[z], gz_s.at[d], gz_r.at[z], along_z(d))

    for h in range(2):
        for d in range(1, 4):
            source = (first[h] + d) % 4
            arrived(r1.at[h, source], p1_r.at[h, source])
        for q in range(4):
            t2[h, q] = r1[h, 0, q] + r1[h, 1, q] + r1[h, 2, q] + r1[h, 3, q]
        for d in range(1, 4):
            q = (second[h] + d) % 4
            send(t2.at[h, q], r2.at[h, second[h]], p2_s.at[h, d], p2_r.at[h, second[h]], along_second[h](d))
        r2[h, second[h]] = t2[h, second[h]]
    for h in range(2):
        for d in range(1, 4):
            source = (second[h] + d) % 4
            arrived(r2.at[h, source], p2_r.at[h, source])
        zb[h, z] = r2[h, 0] + r2[h, 1] + r2[h, 2] + r2[h, 3]
        for d in range(1, NZ):
            send(zb.at[h, z], zb.at[h, z], z_s.at[h, d], z_r.at[h, z], along_z(d))

    for d in range(1, NZ):
        source = (z + d) % NZ
        arrived(gz.at[source], gz_r.at[source])
    packed = gz[0]
    for i in range(1, NZ):
        packed = packed + gz[i]
    gram = jnp.concatenate([packed] + [pltpu.roll(packed, 128 - RANK * b, 1) for b in range(1, 4)], axis=0)
    inverse = inverse_factor(gram)[:, :RANK]
    ov[...] = full_dot(inverse, left, ((1,), (0,)))
    ortho_copy = pltpu.make_async_copy(ov, ortho_out, out_sem.at[2])
    ortho_copy.start()

    base = c * 32
    for h in range(2):
        for d in range(1, NZ):
            source = (z + d) % NZ
            arrived(zb.at[h, source], z_r.at[h, source])
        value = zb[h, 0]
        for i in range(1, NZ):
            value = value + zb[h, i]
        block = base + h * 16 + first[h] * 4 + second[h]
        nb[block] = full_dot(inverse, value, ((1,), (0,)))
        for d in range(1, 4):
            send(nb.at[block], nb.at[block], a2_s.at[h, d], a2_r.at[h, second[h]], along_second[h](d))
    for h in range(2):
        mine = base + h * 16 + first[h] * 4
        for d in range(1, 4):
            source = (second[h] + d) % 4
            arrived(nb.at[mine + source], a2_r.at[h, source])
        rows = pl.ds(mine, 4)
        for d in range(1, 4):
            send(nb.at[rows], nb.at[rows], a1_s.at[h, d], a1_r.at[h, first[h]], along_first[h](d))
        send(nb.at[rows], nb.at[rows], ac_s.at[h, 0], ac_r.at[h, 0], partner)
    for d in range(1, 4):
        for h in range(2):
            source = (first[h] + d) % 4
            rows = pl.ds(base + h * 16 + source * 4, 4)
            arrived(nb.at[rows], a1_r.at[h, source])
            send(nb.at[rows], nb.at[rows], ac_s.at[h, d], ac_r.at[h, d], partner)
    half = pl.ds(base, 32)
    half_copy = pltpu.make_async_copy(nb.at[half], nb_out.at[half], out_sem.at[0])
    half_copy.start()
    for d in range(4):
        for h in range(2):
            source = (first[h] + d) % 4
            rows = pl.ds((1 - c) * 32 + h * 16 + source * 4, 4)
            arrived(nb.at[rows], ac_r.at[h, d])
    other = pl.ds((1 - c) * 32, 32)
    other_copy = pltpu.make_async_copy(nb.at[other], nb_out.at[other], out_sem.at[1])
    other_copy.start()
    for copy in sent:
        copy.wait_send()
    ortho_copy.wait()
    half_copy.wait()
    other_copy.wait()


def apply_kernel(overflow, grad, error, nb, ortho, update, new_error, basis_out):
    width = grad.shape[1]
    health = 1.0 - overflow[0].astype(F32)
    new_basis = jnp.concatenate([nb[i] for i in range(width // 128)], axis=1)
    basis_out[...] = new_basis
    n1, n2, _ = pieces(new_basis)
    o1, o2, _ = pieces(ortho[...])
    approx = lax.dot_general(
        jnp.concatenate([o1, o1, o2], axis=0),
        jnp.concatenate([n1, n2, n1], axis=0),
        (((0,), (0,)), ((), ())),
        preferred_element_type=F32,
    )
    update[...] = approx.astype(BF16)
    error_value = error[...].astype(F32)
    corrected = grad[...].astype(F32) + error_value
    new_error[...] = jnp.where(health > 0.5, corrected - approx, error_value).astype(BF16)


def on_device(grad_out, error_out, basis_out, overflow):
    grad, error = grad_out[0], error_out[0]
    any_spec = pl.BlockSpec(memory_space=pl.ANY)
    dma = pltpu.SemaphoreType.DMA
    vmem = lambda *shape: pltpu.VMEM(shape, F32)
    block = (RANK, 128)
    nb, ortho = pl.pallas_call(
        reduce_kernel,
        out_shape=[jax.ShapeDtypeStruct((64, RANK, 128), F32), jax.ShapeDtypeStruct((RANK, ROWS), F32)],
        in_specs=[any_spec, any_spec, any_spec, pl.BlockSpec(memory_space=pltpu.SMEM)],
        out_specs=[any_spec, any_spec],
        scratch_shapes=[
            pltpu.VMEM((2 * ROWS, D), BF16),
            vmem(RANK, D),
            vmem(2, RANK + 8, 128),
            vmem(NY, RANK + 8, 128),
            vmem(NX, 8, 128),
            vmem(NZ, 8, 128),
            vmem(32, *block),
            vmem(32, *block),
            vmem(32, *block),
            vmem(2, 4, 4, *block),
            vmem(2, 4, *block),
            vmem(2, 4, *block),
            vmem(2, NZ, *block),
            vmem(64, *block),
            vmem(*block),
            dma((3, CHUNKS)),
            dma((1,)), dma((1,)),
            dma((NY,)), dma((NY,)),
            dma((NX,)), dma((NX,)),
            dma((NZ,)), dma((NZ,)),
            dma((8,)), dma((8,)),
            dma((2, 4)), dma((2, 4)),
            dma((2, 4)), dma((2, 4)),
            dma((2, NZ)), dma((2, NZ)),
            dma((2, 4)), dma((2, 4)),
            dma((2, 4)), dma((2, 4)),
            dma((2, 4)), dma((2, 4)),
            dma((3,)),
        ],
        compiler_params=pltpu.CompilerParams(collective_id=0, has_side_effects=True, vmem_limit_bytes=40 << 20),
        name="reduce",
    )(grad, error, basis_out.T, overflow)

    width = 1024
    wide = pl.BlockSpec((ROWS, width), lambda i: (0, i))
    update, new_error, new_basis = pl.pallas_call(
        apply_kernel,
        grid=(D // width,),
        out_shape=[
            jax.ShapeDtypeStruct((ROWS, D), BF16),
            jax.ShapeDtypeStruct((ROWS, D), BF16),
            jax.ShapeDtypeStruct((RANK, D), F32),
        ],
        in_specs=[
            pl.BlockSpec(memory_space=pltpu.SMEM),
            wide,
            wide,
            pl.BlockSpec((width // 128, RANK, 128), lambda i: (i, 0, 0)),
            pl.BlockSpec((RANK, ROWS), lambda i: (0, 0)),
        ],
        out_specs=[wide, wide, pl.BlockSpec((RANK, width), lambda i: (0, i))],
        compiler_params=pltpu.CompilerParams(vmem_limit_bytes=24 << 20),
        name="apply",
    )(overflow, grad, error, nb, ortho)
    return update, new_error[None], new_basis.T


def solution(mesh):
    return jax.shard_map(
        on_device,
        mesh=mesh,
        in_specs=(P("rep", "shard", None), P("rep", "shard", None), P(), P("rep")),
        out_specs=(P("shard", None), P("rep", "shard", None), P()),
        check_vma=False,
    )
```

time: 464 us -> 56.4 us (0.12)
  waiting for transfers between devices: 276 us -> 0 us
  blocking collectives: 144 us -> 0 us
  Pallas kernels: 0 us -> 50.5 us
  matrix products: 18.5 us -> 0 us
  between operations: 15.5 us -> 1.3 us
  other arithmetic: 9.39 us -> 0 us
    psum x1 -> x0, waiting for transfers between devices: 276 us -> none  [on_device(): lax.psum(weight * transpose_project(corrected, ortho), ('rep', 'shard'))]
    psum x2 -> x0, blocking collectives: 144 us -> none  [the longest x1 118 us: orthonormal(): lax.psum(jnp.dot(left.T, left, precision=lax.Precision.HIGHEST), 'shard')]
    pallas_call x0 -> x2, Pallas kernels: none -> 50.5 us  [the longest x1 45.7 us: on_device(): pl.pallas_call(reduce_kernel, out_shape=[jax.ShapeDtypeStruct((64, RANK,...]
    dot_general x4 -> x0, matrix products: 17.6 us -> none  [the longest x1 5.87 us: project(): return jnp.dot(matrix, basis, precision=lax.Precision.HIGHEST)]
    another operation x5 -> x0, other arithmetic: 6.68 us -> none  [the longest x3 3.59 us: orthonormal(): lower = jnp.linalg.cholesky(shifted)]
  transfers between devices with their start and end apart: 1 -> 0, of which waited for: 1 -> 0; matrix products, arithmetic and copies ran while one was open for 0% -> 0% of each run, Pallas kernels for 0% -> 0%
where the time goes in v1:
time: 56.4 us; the launch traced here: 56.2 us
  Pallas kernels  50.5 us (90%)
  local copies, waits for them, and re-layouts  4.4 us (8%)
  between operations  1.3 us (2%)
    pallas_call x1, Pallas kernels, on_device(): pl.pallas_call(reduce_kernel, out_shape=[jax.ShapeDtypeStruct((64, RANK,...  45.7 us
    pallas_call x1, Pallas kernels, on_device(): pl.pallas_call(apply_kernel, grid=(D // width,), out_shape=[jax.ShapeDtyp...  4.87 us
    unnamed x6, local copies, waits for them, and re-layouts  4.4 us

profile of v1, /device:TPU:1, one launch (start us, length us, event | category | flops | bytes accessed | tf_op | source)
XLA Modules:
  0.0 56.2 jit_solution(10206962374961374449)
XLA Ops:
  1.3 0.0 copy-start
  1.3 1.6 %copy-done = bf16[1,128,8192]{2,1,0:T(8,128)(2,1)S(1)} copy-done((bf16[1,128,8192]{2,1,0:T(8,128)(2,1)S(1)}, bf16[1,128,8192]{2,1,0:T(8,128)(2,1)}, u32[]{:S(2)}) %copy-start) | copy-done | bytes 2097176
  2.9 0.0 copy-start.1
  2.9 1.6 %copy-done.1 = bf16[1,128,8192]{2,1,0:T(8,128)(2,1)S(1)} copy-done((bf16[1,128,8192]{2,1,0:T(8,128)(2,1)S(1)}, bf16[1,128,8192]{2,1,0:T(8,128)(2,1)}, u32[]{:S(2)}) %copy-start.1) | copy-done | bytes 2097176
  4.5 0.0 copy-start.2
  4.5 1.2 %copy-done.2 = f32[8192,32]{0,1:T(8,128)S(1)} copy-done((f32[8192,32]{0,1:T(8,128)S(1)}, f32[8192,32]{0,1:T(8,128)}, u32[]{:S(2)}) %copy-start.2) | copy-done | bytes 1048600
  5.7 45.7 %reduce.1 = (f32[64,32,128]{2,1,0:T(8,128)S(1)}, f32[32,128]{1,0:T(8,128)S(1)}) custom-call(bf16[128,8192]{1,0:T(8,128)(2,1)S(1)} %bitcast.5, bf16[128,8192]{1,0:T(8,128)(2,1)S(1)} %bitcast.7, f32[32,8192]{1,0:T(8,128)S(1)} %bitcast.9, s32[1]{0:T(128)S(6)} %copy.7.overflow), custom_call_target="tpu_custom_call" | custom-call | tf_op jit(solution)/shard_map/reduce/pallas_call | solution.py:280
  51.4 4.9 %apply.1 = (bf16[128,8192]{1,0:T(8,128)(2,1)}, bf16[128,8192]{1,0:T(8,128)(2,1)}, f32[32,8192]{1,0:T(8,128)}) custom-call(s32[1]{0:T(128)S(6)} %copy.7.overflow, bf16[128,8192]{1,0:T(8,128)(2,1)S(1)} %bitcast.6, bf16[128,8192]{1,0:T(8,128)(2,1)S(1)} %bitcast.8, f32[64,32,128]{2,1,0:T(8,128)S(1)} %get-tuple-element.8.nb, f32[32,128]{1,0:T(8,128)S(1)} %get-tuple-element.9.ortho), custom_call_target="tpu_custom_call" | custom-call | tf_op jit(solution)/shard_map/apply/pallas_call | solution.py:321
Async XLA Ops:
  1.3 1.6 %copy-start = (bf16[1,128,8192]{2,1,0:T(8,128)(2,1)S(1)}, bf16[1,128,8192]{2,1,0:T(8,128)(2,1)}, u32[]{:S(2)}) copy-start(bf16[1,128,8192]{2,1,0:T(8,128)(2,1)} %param.4) | copy-start | bytes 6291460
  2.9 1.6 %copy-start.1 = (bf16[1,128,8192]{2,1,0:T(8,128)(2,1)S(1)}, bf16[1,128,8192]{2,1,0:T(8,128)(2,1)}, u32[]{:S(2)}) copy-start(bf16[1,128,8192]{2,1,0:T(8,128)(2,1)} %param.5) | copy-start | bytes 6291460
  4.5 1.2 %copy-start.2 = (f32[8192,32]{0,1:T(8,128)S(1)}, f32[8192,32]{0,1:T(8,128)}, u32[]{:S(2)}) copy-start(f32[8192,32]{0,1:T(8,128)} %param.6) | copy-start | bytes 3145732

commit v2 on v1

--- a/solution.py
+++ b/solution.py
@@ -10,9 +10,10 @@
 MESH = pl.DeviceIdType.MESH
 F32, BF16 = jnp.float32, jnp.bfloat16
 D, RANK, ROWS = 8192, 32, 128
-CHUNKS = 4
+CHUNKS, AHEAD = 8, 3
 CHUNK = D // CHUNKS
 NY, NX, NZ = 4, 4, 8
+WIDTH = 1024
 
 
 def pieces(value):
@@ -45,10 +46,10 @@
 
 
 def reduce_kernel(
-    grad_hbm, error_hbm, basis_hbm, overflow, nb_out, ortho_out,
-    ge, bt, lc, ly, gx, gz, sp, rc, t1, r1, t2, r2, zb, nb, ov,
+    grad_hbm, error_hbm, basis_hbm, overflow, nb, ortho, ge,
+    bt, lc, ly, gx, gz, sp, rc, t1, r1, t2, r2, zb,
     in_sem, lc_s, lc_r, ly_s, ly_r, gx_s, gx_r, gz_s, gz_r, rc_s, rc_r,
-    p1_s, p1_r, p2_s, p2_r, z_s, z_r, a2_s, a2_r, a1_s, a1_r, ac_s, ac_r, out_sem,
+    p1_s, p1_r, p2_s, p2_r, z_s, z_r, a2_s, a2_r, a1_s, a1_r, ac_s, ac_r, ag_s, ag_r,
 ):
     rep, shard = lax.axis_index("rep"), lax.axis_index("shard")
     y, c = rep // 2, rep % 2
@@ -83,17 +84,18 @@
     def arrived(dst, recv_sem):
         remote(dst, dst, lc_s.at[0], recv_sem, partner).wait_recv()
 
-    loads = []
-    for k in range(CHUNKS):
+    def load(k):
         cols = pl.ds(k * CHUNK, CHUNK)
-        group = [
+        return [
             pltpu.make_async_copy(basis_hbm.at[:, cols], bt.at[:, cols], in_sem.at[0, k]),
             pltpu.make_async_copy(grad_hbm.at[:, cols], ge.at[pl.ds(0, ROWS), cols], in_sem.at[1, k]),
             pltpu.make_async_copy(error_hbm.at[:, cols], ge.at[pl.ds(ROWS, ROWS), cols], in_sem.at[2, k]),
         ]
-        for copy in group:
+
+    loads = [load(k) for k in range(CHUNKS)]
+    for k in range(AHEAD):
+        for copy in loads[k]:
             copy.start()
-        loads.append(group)
 
     barrier = pltpu.get_barrier_semaphore()
     others = [partner]
@@ -107,6 +109,9 @@
     for k in range(CHUNKS):
         for copy in loads[k]:
             copy.wait()
+        if k + AHEAD < CHUNKS:
+            for copy in loads[k + AHEAD]:
+                copy.start()
         cols = pl.ds(k * CHUNK, CHUNK)
         basis = jnp.concatenate(pieces(bt[:, cols]), axis=0)
         acc += lax.dot_general(basis, ge[:, cols], (((1,), (1,)), ((), ())), preferred_element_type=F32)
@@ -149,7 +154,7 @@
     second = (y, x)
     along_first = (along_x, along_y)
     along_second = (along_y, along_x)
-    order = [(d, h) for d in (1, 2, 3, 0) for h in range(2)]
+    order = [(d, h) for h in range(2) for d in (1, 2, 3, 0)]
     for i, (d, h) in enumerate(order):
         group = h * 16 + ((first[h] + d) % 4) * 4
         theirs = (1 - c) * 32 + group
@@ -203,11 +208,14 @@
         packed = packed + gz[i]
     gram = jnp.concatenate([packed] + [pltpu.roll(packed, 128 - RANK * b, 1) for b in range(1, 4)], axis=0)
     inverse = inverse_factor(gram)[:, :RANK]
-    ov[...] = full_dot(inverse, left, ((1,), (0,)))
-    ortho_copy = pltpu.make_async_copy(ov, ortho_out, out_sem.at[2])
-    ortho_copy.start()
-
-    base = c * 32
+    ortho[...] = full_dot(inverse, left, ((1,), (0,)))
+
+    def forward(h, p, q):
+        block = c * 32 + h * 16 + p * 4 + q
+        for d in (1, 3, 2):
+            send(nb.at[block], nb.at[block], a1_s.at[h, d, q], a1_r.at[h, p, q], along_first[h](d))
+        send(nb.at[block], nb.at[block], ac_s.at[h, 0, q], ac_r.at[h, p, q], partner)
+
     for h in range(2):
         for d in range(1, NZ):
             source = (z + d) % NZ
@@ -215,75 +223,84 @@
         value = zb[h, 0]
         for i in range(1, NZ):
             value = value + zb[h, i]
-        block = base + h * 16 + first[h] * 4 + second[h]
+        block = c * 32 + h * 16 + first[h] * 4 + second[h]
         nb[block] = full_dot(inverse, value, ((1,), (0,)))
-        for d in range(1, 4):
+        for d in (1, 3, 2):
             send(nb.at[block], nb.at[block], a2_s.at[h, d], a2_r.at[h, second[h]], along_second[h](d))
+        forward(h, first[h], second[h])
+    for d in (1, 3, 2):
+        for h in range(2):
+            q = (second[h] + d) % 4
+            block = c * 32 + h * 16 + first[h] * 4 + q
+            arrived(nb.at[block], a2_r.at[h, q])
+            forward(h, first[h], q)
+    for d in (1, 3, 2):
+        for h in range(2):
+            p = (first[h] + d) % 4
+            for k in range(4):
+                q = (second[h] + (0, 1, 3, 2)[k]) % 4
+                block = c * 32 + h * 16 + p * 4 + q
+                arrived(nb.at[block], a1_r.at[h, p, q])
+            rows = pl.ds(c * 32 + h * 16 + p * 4, 4)
+            send(nb.at[rows], nb.at[rows], ag_s.at[h, d], ag_r.at[h, p], partner)
     for h in range(2):
-        mine = base + h * 16 + first[h] * 4
-        for d in range(1, 4):
-            source = (second[h] + d) % 4
-            arrived(nb.at[mine + source], a2_r.at[h, source])
-        rows = pl.ds(mine, 4)
-        for d in range(1, 4):
-            send(nb.at[rows], nb.at[rows], a1_s.at[h, d], a1_r.at[h, first[h]], along_first[h](d))
-        send(nb.at[rows], nb.at[rows], ac_s.at[h, 0], ac_r.at[h, 0], partner)
-    for d in range(1, 4):
-        for h in range(2):
-            source = (first[h] + d) % 4
-            rows = pl.ds(base + h * 16 + source * 4, 4)
-            arrived(nb.at[rows], a1_r.at[h, source])
-            send(nb.at[rows], nb.at[rows], ac_s.at[h, d], ac_r.at[h, d], partner)
-    half = pl.ds(base, 32)
-    half_copy = pltpu.make_async_copy(nb.at[half], nb_out.at[half], out_sem.at[0])
-    half_copy.start()
-    for d in range(4):
-        for h in range(2):
-            source = (first[h] + d) % 4
-            rows = pl.ds((1 - c) * 32 + h * 16 + source * 4, 4)
-            arrived(nb.at[rows], ac_r.at[h, d])
-    other = pl.ds((1 - c) * 32, 32)
-    other_copy = pltpu.make_async_copy(nb.at[other], nb_out.at[other], out_sem.at[1])
-    other_copy.start()
+        theirs = (1 - c) * 32 + h * 16
+        for q in range(4):
+            arrived(nb.at[theirs + first[h] * 4 + q], ac_r.at[h, first[h], q])
+        for d in (1, 3, 2):
+            p = (first[h] + d) % 4
+            arrived(nb.at[pl.ds(theirs + p * 4, 4)], ag_r.at[h, p])
     for copy in sent:
         copy.wait_send()
-    ortho_copy.wait()
-    half_copy.wait()
-    other_copy.wait()
-
-
-def apply_kernel(overflow, grad, error, nb, ortho, update, new_error, basis_out):
-    width = grad.shape[1]
+
+
+def apply_kernel(overflow, ge, nb, ortho, update_hbm, error_hbm, basis_hbm, update, new_error, basis, sem):
     health = 1.0 - overflow[0].astype(F32)
-    new_basis = jnp.concatenate([nb[i] for i in range(width // 128)], axis=1)
-    basis_out[...] = new_basis
-    n1, n2, _ = pieces(new_basis)
     o1, o2, _ = pieces(ortho[...])
-    approx = lax.dot_general(
-        jnp.concatenate([o1, o1, o2], axis=0),
-        jnp.concatenate([n1, n2, n1], axis=0),
-        (((0,), (0,)), ((), ())),
-        preferred_element_type=F32,
-    )
-    update[...] = approx.astype(BF16)
-    error_value = error[...].astype(F32)
-    corrected = grad[...].astype(F32) + error_value
-    new_error[...] = jnp.where(health > 0.5, corrected - approx, error_value).astype(BF16)
+    ortho_pieces = jnp.concatenate([o1, o1, o2], axis=0)
+    copies = []
+    for k in range(D // WIDTH):
+        cols = pl.ds(k * WIDTH, WIDTH)
+        count = WIDTH // 128
+        new_basis = jnp.concatenate([nb[k * count + i] for i in range(count)], axis=1)
+        basis[:, cols] = new_basis
+        n1, n2, _ = pieces(new_basis)
+        approx = lax.dot_general(
+            ortho_pieces,
+            jnp.concatenate([n1, n2, n1], axis=0),
+            (((0,), (0,)), ((), ())),
+            preferred_element_type=F32,
+        )
+        update[:, cols] = approx.astype(BF16)
+        error_value = ge[ROWS:, cols].astype(F32)
+        corrected = ge[:ROWS, cols].astype(F32) + error_value
+        new_error[:, cols] = jnp.where(health > 0.5, corrected - approx, error_value).astype(BF16)
+        for i, (value, out) in enumerate(((basis, basis_hbm), (update, update_hbm), (new_error, error_hbm))):
+            copy = pltpu.make_async_copy(value.at[:, cols], out.at[:, cols], sem.at[i, k])
+            copy.start()
+            copies.append(copy)
+    for copy in copies:
+        copy.wait()
 
 
 def on_device(grad_out, error_out, basis_out, overflow):
     grad, error = grad_out[0], error_out[0]
-    any_spec = pl.BlockSpec(memory_space=pl.ANY)
+    hbm = pl.BlockSpec(memory_space=pltpu.MemorySpace.HBM)
+    smem, whole = pl.BlockSpec(memory_space=pltpu.SMEM), pl.BlockSpec(memory_space=pltpu.VMEM)
     dma = pltpu.SemaphoreType.DMA
     vmem = lambda *shape: pltpu.VMEM(shape, F32)
     block = (RANK, 128)
-    nb, ortho = pl.pallas_call(
+    operands = [pltpu.with_memory_space_constraint(a, pltpu.HBM) for a in (grad, error, basis_out.T)]
+    nb, ortho, ge = pl.pallas_call(
         reduce_kernel,
-        out_shape=[jax.ShapeDtypeStruct((64, RANK, 128), F32), jax.ShapeDtypeStruct((RANK, ROWS), F32)],
-        in_specs=[any_spec, any_spec, any_spec, pl.BlockSpec(memory_space=pltpu.SMEM)],
-        out_specs=[any_spec, any_spec],
+        out_shape=[
+            vmem(64, *block),
+            vmem(RANK, ROWS),
+            pltpu.VMEM((2 * ROWS, D), BF16),
+        ],
+        in_specs=[hbm, hbm, hbm, smem],
+        out_specs=[whole, whole, whole],
         scratch_shapes=[
-            pltpu.VMEM((2 * ROWS, D), BF16),
             vmem(RANK, D),
             vmem(2, RANK + 8, 128),
             vmem(NY, RANK + 8, 128),
@@ -296,8 +313,6 @@
             vmem(2, 4, *block),
             vmem(2, 4, *block),
             vmem(2, NZ, *block),
-            vmem(64, *block),
-            vmem(*block),
             dma((3, CHUNKS)),
             dma((1,)), dma((1,)),
             dma((NY,)), dma((NY,)),
@@ -308,35 +323,29 @@
             dma((2, 4)), dma((2, 4)),
             dma((2, NZ)), dma((2, NZ)),
             dma((2, 4)), dma((2, 4)),
+            dma((2, 4, 4)), dma((2, 4, 4)),
+            dma((2, 1, 4)), dma((2, 4, 4)),
             dma((2, 4)), dma((2, 4)),
-            dma((2, 4)), dma((2, 4)),
-            dma((3,)),
         ],
-        compiler_params=pltpu.CompilerParams(collective_id=0, has_side_effects=True, vmem_limit_bytes=40 << 20),
+        compiler_params=pltpu.CompilerParams(collective_id=0, has_side_effects=True, vmem_limit_bytes=32 << 20),
         name="reduce",
-    )(grad, error, basis_out.T, overflow)
-
-    width = 1024
-    wide = pl.BlockSpec((ROWS, width), lambda i: (0, i))
+    )(*operands, overflow)
+
     update, new_error, new_basis = pl.pallas_call(
         apply_kernel,
-        grid=(D // width,),
         out_shape=[
             jax.ShapeDtypeStruct((ROWS, D), BF16),
             jax.ShapeDtypeStruct((ROWS, D), BF16),
             jax.ShapeDtypeStruct((RANK, D), F32),
         ],
-        in_specs=[
-            pl.BlockSpec(memory_space=pltpu.SMEM),
-            wide,
-            wide,
-            pl.BlockSpec((width // 128, RANK, 128), lambda i: (i, 0, 0)),
-            pl.BlockSpec((RANK, ROWS), lambda i: (0, 0)),
+        in_specs=[smem, whole, whole, whole],
+        out_specs=[hbm, hbm, hbm],
+        scratch_shapes=[
+            pltpu.VMEM((ROWS, D), BF16), pltpu.VMEM((ROWS, D), BF16), vmem(RANK, D), dma((3, D // WIDTH))
         ],
-        out_specs=[wide, wide, pl.BlockSpec((RANK, width), lambda i: (0, i))],
         compiler_params=pltpu.CompilerParams(vmem_limit_bytes=24 << 20),
         name="apply",
-    )(overflow, grad, error, nb, ortho)
+    )(overflow, ge, nb, ortho)
     return update, new_error[None], new_basis.T
 
 

time: 56.4 us -> 51.3 us (0.910)
  local copies, waits for them, and re-layouts: 4.4 us -> 0 us
  Pallas kernels: 50.5 us -> 49.8 us
    unnamed x6 -> x0, local copies, waits for them, and re-layouts: 4.4 us -> none
    pallas_call x2, Pallas kernels: 50.5 us -> 49.8 us  [the longest x1 47 us: on_device(): pl.pallas_call(reduce_kernel, out_shape=[vmem(64, *block), vmem(RANK, ROW...]
where the time goes in v2:
time: 51.3 us; the launch traced here: 51.1 us
  Pallas kernels  49.8 us (97%)
  between operations  1.29 us (3%)
    pallas_call x1, Pallas kernels, on_device(): pl.pallas_call(reduce_kernel, out_shape=[vmem(64, *block), vmem(RANK, ROW...  47 us
    pallas_call x1, Pallas kernels, on_device(): pl.pallas_call(apply_kernel, out_shape=[jax.ShapeDtypeStruct((ROWS, D), B...  2.83 us

profile of v2, /device:TPU:1, one launch (start us, length us, event | category | flops | bytes accessed | tf_op | source)
XLA Modules:
  0.0 51.1 jit_solution(13017062577589279868)
XLA Ops:
  1.3 47.0 %reduce.1 = (f32[64,32,128]{2,1,0:T(8,128)S(1)}, f32[32,128]{1,0:T(8,128)S(1)}, bf16[256,8192]{1,0:T(8,128)(2,1)S(1)}) custom-call(bf16[128,8192]{1,0:T(8,128)(2,1)} %bitcast.5, bf16[128,8192]{1,0:T(8,128)(2,1)} %bitcast.6, f32[32,8192]{1,0:T(8,128)} %bitcast.7, s32[1]{0:T(128)S(6)} %copy.7.overflow), custom_call_target="tpu_custom_call" | custom-call | tf_op jit(solution)/shard_map/reduce/pallas_call | solution.py:294
  48.3 2.8 %apply.1 = (bf16[128,8192]{1,0:T(8,128)(2,1)}, bf16[128,8192]{1,0:T(8,128)(2,1)}, f32[32,8192]{1,0:T(8,128)}) custom-call(s32[1]{0:T(128)S(6)} %copy.7.overflow, bf16[256,8192]{1,0:T(8,128)(2,1)S(1)} %get-tuple-element.9.ge, f32[64,32,128]{2,1,0:T(8,128)S(1)} %get-tuple-element.10.nb, f32[32,128]{1,0:T(8,128)S(1)} %get-tuple-element.11.ortho), custom_call_target="tpu_custom_call" | custom-call | tf_op jit(solution)/shard_map/apply/pallas_call | solution.py:334

commit v3 on v2

v3 whole, which is shorter than its diff:
```python
import functools

import jax
import jax.numpy as jnp
from jax import lax
from jax.experimental import pallas as pl
from jax.experimental.pallas import tpu as pltpu
from jax.sharding import PartitionSpec as P

MESH = pl.DeviceIdType.MESH
F32, BF16 = jnp.float32, jnp.bfloat16
D, RANK, ROWS = 8192, 32, 128
HALF, MPARTS = D // 2, 4
NY, NX, NZ = 4, 4, 8
WIDTH = 1024


def pieces(value):
    first = value.astype(BF16)
    rest = value - first.astype(F32)
    second = rest.astype(BF16)
    third = (rest - second.astype(F32)).astype(BF16)
    return first, second, third


def full_dot(a, b, dims):
    return lax.dot_general(a, b, (dims, ((), ())), precision=lax.Precision.HIGHEST, preferred_element_type=F32)


def inverse_factor(gram):
    row = lax.broadcasted_iota(jnp.int32, (RANK, 128), 0)
    lane = lax.broadcasted_iota(jnp.int32, (RANK, 128), 1)
    diagonal = row == lane
    trace = jnp.sum(jnp.where(diagonal, gram, 0.0), axis=(0, 1), keepdims=True)
    shift = 1e-05 * (trace / RANK)
    work = jnp.where(lane < RANK, gram, 0.0) + jnp.where(diagonal, shift, 0.0)
    work = work + jnp.where(lane - RANK == row, 1.0, 0.0)
    for j in range(RANK - 1):
        column = jnp.broadcast_to(work[:, j : j + 1], (RANK, 128))
        scaled = work[j : j + 1, :] / column[j : j + 1, :]
        work = work - jnp.where(row > j, column, 0.0) * scaled
    pivots = jnp.sum(jnp.where(diagonal, work, 0.0), axis=1, keepdims=True)
    inverse = work * lax.rsqrt(pivots)
    return pltpu.roll(inverse, 128 - RANK, 1)


def reduce_kernel(
    grad_hbm, error_hbm, basis_hbm, overflow, nb, ortho, ge,
    bt, hb, mo, mi, mc, ly, gx, gz, t1, r1, t2, r2, zb,
    in_sem, m_r, ly_r, gx_r, gz_r, p1_r, p2_r, z_r, a2_r, a1_r, ac_r, s_sem,
):
    rep, shard = lax.axis_index("rep"), lax.axis_index("shard")
    y, c = rep // 2, rep % 2
    x, z = shard // NZ, shard % NZ

    def at(y_, c_, x_, z_):
        return (y_ * 2 + c_, x_ * NZ + z_)

    partner = at(y, 1 - c, x, z)

    def along_y(d):
        return at((y + d) % NY, c, x, z)

    def along_x(d):
        return at(y, c, (x + d) % NX, z)

    def along_z(d):
        return at(y, c, x, (z + d) % NZ)

    def remote(src, dst, send, recv, device):
        return pltpu.make_async_remote_copy(
            src_ref=src, dst_ref=dst, send_sem=send, recv_sem=recv, device_id=device, device_id_type=MESH
        )

    def send(src, dst, phase, recv_sem, device):
        remote(src, dst, s_sem.at[phase], recv_sem, device).start()

    def arrived(like, recv_sem):
        remote(like, like, s_sem.at[0], recv_sem, partner).wait_recv()

    def all_sent(like, phase):
        remote(like, like, s_sem.at[phase], m_r.at[0], partner).wait_send()

    def blocks(count):
        return nb.at[pl.ds(0, count)]

    halves = [(1 - c) * HALF, c * HALF]
    loads = []
    for i, start in enumerate(halves):
        cols = pl.ds(pl.multiple_of(start, HALF), HALF)
        group = [
            pltpu.make_async_copy(grad_hbm.at[:, cols], ge.at[pl.ds(0, ROWS), cols], in_sem.at[0, i]),
            pltpu.make_async_copy(error_hbm.at[:, cols], ge.at[pl.ds(ROWS, ROWS), cols], in_sem.at[1, i]),
            pltpu.make_async_copy(basis_hbm.at[:, cols], bt.at[:, cols], in_sem.at[2, i]),
        ]
        for copy in group:
            copy.start()
        loads.append(group)

    barrier = pltpu.get_barrier_semaphore()
    replicas = [(2, 0), (2, 1), (1, 0), (3, 0), (1, 1), (3, 1), (0, 1)]
    replicas = [at((y + dy) % NY, (c + dc) % 2, x, z) for dy, dc in replicas]
    others = replicas + [along_x(d) for d in range(1, NX)] + [along_z(d) for d in range(1, NZ)]
    for other in others:
        pl.semaphore_signal(barrier, inc=1, device_id=other, device_id_type=MESH)

    health = jnp.full((8, 128), 1.0 - overflow[0].astype(F32), F32)
    hb[0] = health
    weight = health[:1, :1]

    def corrected(start):
        cols = pl.ds(pl.multiple_of(start, 512), 512)
        return (ge[:ROWS, cols].astype(F32) + ge[ROWS:, cols].astype(F32)) * weight

    def project(start):
        cols = pl.ds(pl.multiple_of(start, 512), 1024)
        basis = jnp.concatenate(pieces(bt[:, cols]), axis=0)
        return lax.dot_general(basis, ge[:, cols], (((1,), (1,)), ((), ())), preferred_element_type=F32)

    for copy in loads[0]:
        copy.wait()
    acc = jnp.zeros((3 * RANK, 2 * ROWS), F32)
    for k in range(HALF // 1024):
        acc += project(halves[0] + k * 1024)
        for i in range(2):
            mo[:, pl.ds(k * 1024 + i * 512, 512)] = corrected(halves[0] + k * 1024 + i * 512)
    pl.semaphore_wait(barrier, len(others))
    send(hb.at[0], hb.at[1], 0, m_r.at[MPARTS], partner)
    for k in range(MPARTS):
        rows = pl.ds(k * (ROWS // MPARTS), ROWS // MPARTS)
        send(mo.at[rows], mi.at[rows], 1, m_r.at[k], partner)
    for copy in loads[1]:
        copy.wait()
    for k in range(HALF // 1024):
        acc += project(halves[1] + k * 1024)
    both = acc[:RANK] + acc[RANK : 2 * RANK] + acc[2 * RANK :]

    ly[rep] = (both[:, :ROWS] + both[:, ROWS:]) * weight
    for other in replicas:
        send(ly.at[rep], ly.at[rep], 2, ly_r.at[0], other)

    for k in range(MPARTS):
        size = ROWS // MPARTS
        rows = pl.ds(k * size, size)
        arrived(mi.at[rows], m_r.at[k])
        for i in range(HALF // 1024):
            own = pl.ds(pl.multiple_of(halves[1] + i * 1024, 1024), 1024)
            cols = pl.ds(i * 1024, 1024)
            value = ge[rows, own].astype(F32) + ge[pl.ds(ROWS + k * size, size), own].astype(F32)
            value = value * weight + mi[rows, cols]
            high = value.astype(BF16)
            mc[rows, cols] = high
            mc[pl.ds(ROWS + k * size, size), cols] = (value - high.astype(F32)).astype(BF16)
    arrived(hb.at[1], m_r.at[MPARTS])
    count = hb[0] + hb[1]

    arrived(ly.at[pl.ds(0, 7)], ly_r.at[0])
    left = ly[0]
    for i in range(1, 8):
        left = left + ly[i]

    weighted = jnp.concatenate(pieces(left), axis=0)
    weighted = jnp.concatenate([weighted, weighted], axis=1)
    first = (x, y)
    second = (y, x)
    along_first = (along_x, along_y)
    along_second = (along_y, along_x)
    for d in (2, 1, 3, 0):
        for h in range(2):
            p = (first[h] + d) % 4
            group = h * 16 + p * 4
            cols = pl.ds(pl.multiple_of(group * 128, 512), 512)
            out = lax.dot_general(weighted, mc[:, cols], (((1,), (0,)), ((), ())), preferred_element_type=F32)
            value = out[:RANK] + out[RANK : 2 * RANK] + out[2 * RANK :]
            for q in range(4):
                part = value[:, q * 128 : (q + 1) * 128]
                if d == 0:
                    r1[h, p, q] = part
                else:
                    t1[group + q] = part
            if d:
                send(t1.at[pl.ds(group, 4)], r1.at[h, first[h]], 3, p1_r.at[h], along_first[h](d))

    gram = full_dot(left, jnp.concatenate([left] * 4, axis=0), ((1,), (1,)))
    lane_group = lax.broadcasted_iota(jnp.int32, (8, 128), 1) // RANK
    packed = gram[:8]
    for b in range(1, 4):
        packed = jnp.where(lane_group == b, gram[8 * b : 8 * b + 8], packed)
    gx[x] = packed
    for d in (2, 1, 3):
        send(gx.at[x], gx.at[x], 4, gx_r.at[0], along_x(d))
    all_sent(hb.at[0], 0)
    all_sent(mo, 1)
    all_sent(blocks(7), 2)
    arrived(gx.at[pl.ds(0, 3)], gx_r.at[0])
    gz[z] = gx[0] + gx[1] + gx[2] + gx[3]
    for d in (4, 3, 5, 2, 6, 1, 7):
        send(gz.at[z], gz.at[z], 5, gz_r.at[0], along_z(d))

    for h in range(2):
        arrived(blocks(12), p1_r.at[h])
        for q in range(4):
            t2[h * 4 + q, :RANK] = r1[h, 0, q] + r1[h, 1, q] + r1[h, 2, q] + r1[h, 3, q]
            t2[h * 4 + q, RANK:] = count
        for d in (2, 1, 3):
            q = (second[h] + d) % 4
            send(t2.at[h * 4 + q], r2.at[h * 4 + second[h]], 6, p2_r.at[h], along_second[h](d))
        r2[h * 4 + second[h]] = t2[h * 4 + second[h]]
    for h in range(2):
        arrived(r2.at[pl.ds(0, 3)], p2_r.at[h])
    for h in range(2):
        zb[z, h] = r2[h * 4, :RANK] + r2[h * 4 + 1, :RANK] + r2[h * 4 + 2, :RANK] + r2[h * 4 + 3, :RANK]
    for d in (4, 3, 5, 2, 6, 1, 7):
        send(zb.at[z], zb.at[z], 7, z_r.at[0], along_z(d))
    kept = r2[0, RANK:] + r2[1, RANK:] + r2[2, RANK:] + r2[3, RANK:]

    all_sent(blocks(24), 3)
    all_sent(gx.at[pl.ds(0, 3)], 4)
    all_sent(gz.at[pl.ds(0, 7)], 5)
    arrived(gz.at[pl.ds(0, 7)], gz_r.at[0])
    packed = gz[0]
    for i in range(1, NZ):
        packed = packed + gz[i]
    gram = jnp.concatenate([packed] + [pltpu.roll(packed, 128 - RANK * b, 1) for b in range(1, 4)], axis=0)
    inverse = inverse_factor(gram)[:, :RANK]
    ortho[...] = full_dot(inverse, left, ((1,), (0,)))
    all_sent(r2.at[pl.ds(0, 6)], 6)

    arrived(zb.at[pl.ds(0, 7)], z_r.at[0])
    base = c * 32
    for h in range(2):
        value = zb[0, h]
        for i in range(1, NZ):
            value = value + zb[i, h]
        block = base + h * 16 + first[h] * 4 + second[h]
        nb[block] = full_dot(inverse, value, ((1,), (0,))) / kept[:1]
        for d in (2, 1, 3):
            send(nb.at[block], nb.at[block], 8, a2_r.at[h], along_second[h](d))
    for h in range(2):
        arrived(blocks(3), a2_r.at[h])
        rows = pl.ds(base + h * 16 + first[h] * 4, 4)
        for d in (2, 1, 3):
            send(nb.at[rows], nb.at[rows], 9, a1_r.at[h, first[h]], along_first[h](d))
        send(nb.at[rows], nb.at[rows], 10, ac_r.at[0], partner)
    all_sent(blocks(14), 7)
    all_sent(blocks(6), 8)
    for d in (1, 3, 2):
        for h in range(2):
            p = (first[h] + d) % 4
            rows = pl.ds(base + h * 16 + p * 4, 4)
            arrived(nb.at[rows], a1_r.at[h, p])
            send(nb.at[rows], nb.at[rows], 10, ac_r.at[0], partner)
    all_sent(blocks(24), 9)
    arrived(blocks(32), ac_r.at[0])
    all_sent(blocks(32), 10)


def apply_kernel(overflow, ge, nb, ortho, update_hbm, error_hbm, basis_hbm, update, new_error, basis, sem):
    health = 1.0 - overflow[0].astype(F32)
    o1, o2, _ = pieces(ortho[...])
    ortho_pieces = jnp.concatenate([o1, o1, o2], axis=0)
    copies = []
    for k in range(D // WIDTH):
        cols = pl.ds(k * WIDTH, WIDTH)
        count = WIDTH // 128
        new_basis = jnp.concatenate([nb[k * count + i] for i in range(count)], axis=1)
        basis[:, cols] = new_basis
        n1, n2, _ = pieces(new_basis)
        approx = lax.dot_general(
            ortho_pieces,
            jnp.concatenate([n1, n2, n1], axis=0),
            (((0,), (0,)), ((), ())),
            preferred_element_type=F32,
        )
        update[:, cols] = approx.astype(BF16)
        error_value = ge[ROWS:, cols].astype(F32)
        corrected = ge[:ROWS, cols].astype(F32) + error_value
        new_error[:, cols] = jnp.where(health > 0.5, corrected - approx, error_value).astype(BF16)
        for i, (value, out) in enumerate(((basis, basis_hbm), (update, update_hbm), (new_error, error_hbm))):
            copy = pltpu.make_async_copy(value.at[:, cols], out.at[:, cols], sem.at[i, k])
            copy.start()
            copies.append(copy)
    for copy in copies:
        copy.wait()


def on_device(grad_out, error_out, basis_out, overflow):
    grad, error = grad_out[0], error_out[0]
    hbm = pl.BlockSpec(memory_space=pltpu.MemorySpace.HBM)
    smem, whole = pl.BlockSpec(memory_space=pltpu.SMEM), pl.BlockSpec(memory_space=pltpu.VMEM)
    dma = pltpu.SemaphoreType.DMA
    vmem = lambda *shape: pltpu.VMEM(shape, F32)
    block = (RANK, 128)
    operands = [pltpu.with_memory_space_constraint(a, pltpu.HBM) for a in (grad, error, basis_out.T)]
    nb, ortho, ge = pl.pallas_call(
        reduce_kernel,
        out_shape=[
            vmem(64, *block),
            vmem(RANK, ROWS),
            pltpu.VMEM((2 * ROWS, D), BF16),
        ],
        in_specs=[hbm, hbm, hbm, smem],
        out_specs=[whole, whole, whole],
        scratch_shapes=[
            vmem(RANK, D),
            vmem(2, 8, 128),
            vmem(ROWS, HALF),
            vmem(ROWS, HALF),
            pltpu.VMEM((2 * ROWS, HALF), BF16),
            vmem(8, *block),
            vmem(NX, 8, 128),
            vmem(NZ, 8, 128),
            vmem(32, *block),
            vmem(2, 4, 4, *block),
            vmem(8, RANK + 8, 128),
            vmem(8, RANK + 8, 128),
            vmem(NZ, 2, *block),
            dma((3, 2)),
            dma((MPARTS + 1,)),
            dma((1,)),
            dma((1,)),
            dma((1,)),
            dma((2,)),
            dma((2,)),
            dma((1,)),
            dma((2,)),
            dma((2, 4)),
            dma((1,)),
            dma((11,)),
        ],
        compiler_params=pltpu.CompilerParams(collective_id=0, has_side_effects=True, vmem_limit_bytes=32 << 20),
        name="reduce",
    )(*operands, overflow)

    update, new_error, new_basis = pl.pallas_call(
        apply_kernel,
        out_shape=[
            jax.ShapeDtypeStruct((ROWS, D), BF16),
            jax.ShapeDtypeStruct((ROWS, D), BF16),
            jax.ShapeDtypeStruct((RANK, D), F32),
        ],
        in_specs=[smem, whole, whole, whole],
        out_specs=[hbm, hbm, hbm],
        scratch_shapes=[
            pltpu.VMEM((ROWS, D), BF16), pltpu.VMEM((ROWS, D), BF16), vmem(RANK, D), dma((3, D // WIDTH))
        ],
        compiler_params=pltpu.CompilerParams(vmem_limit_bytes=24 << 20),
        name="apply",
    )(overflow, ge, nb, ortho)
    return update, new_error[None], new_basis.T


def solution(mesh):
    return jax.shard_map(
        on_device,
        mesh=mesh,
        in_specs=(P("rep", "shard", None), P("rep", "shard", None), P(), P("rep")),
        out_specs=(P("shard", None), P("rep", "shard", None), P()),
        check_vma=False,
    )
```

time: 51.3 us -> 47 us (0.916)
  Pallas kernels: 49.8 us -> 45.7 us
    pallas_call x1, Pallas kernels: 47 us -> 42.9 us  [on_device(): pl.pallas_call(reduce_kernel, out_shape=[vmem(64, *block), vmem(RANK, ROW...]
where the time goes in v3:
time: 47 us
  Pallas kernels  45.7 us (97%)
  between operations  1.29 us (3%)
    pallas_call x1, Pallas kernels, on_device(): pl.pallas_call(reduce_kernel, out_shape=[vmem(64, *block), vmem(RANK, ROW...  42.9 us
    pallas_call x1, Pallas kernels, on_device(): pl.pallas_call(apply_kernel, out_shape=[jax.ShapeDtypeStruct((ROWS, D), B...  2.81 us

profile of v3, /device:TPU:1, one launch (start us, length us, event | category | flops | bytes accessed | tf_op | source)
XLA Modules:
  0.0 47.0 jit_solution(13537834829350916107)
XLA Ops:
  1.3 42.9 %reduce.1 = (f32[64,32,128]{2,1,0:T(8,128)S(1)}, f32[32,128]{1,0:T(8,128)S(1)}, bf16[256,8192]{1,0:T(8,128)(2,1)S(1)}) custom-call(bf16[128,8192]{1,0:T(8,128)(2,1)} %bitcast.5, bf16[128,8192]{1,0:T(8,128)(2,1)} %bitcast.6, f32[32,8192]{1,0:T(8,128)} %bitcast.7, s32[1]{0:T(128)S(6)} %copy.7.overflow), custom_call_target="tpu_custom_call" | custom-call | tf_op jit(solution)/shard_map/reduce/pallas_call | solution.py:295
  44.1 2.8 %apply.1 = (bf16[128,8192]{1,0:T(8,128)(2,1)}, bf16[128,8192]{1,0:T(8,128)(2,1)}, f32[32,8192]{1,0:T(8,128)}) custom-call(s32[1]{0:T(128)S(6)} %copy.7.overflow, bf16[256,8192]{1,0:T(8,128)(2,1)S(1)} %get-tuple-element.9.ge, f32[64,32,128]{2,1,0:T(8,128)S(1)} %get-tuple-element.10.nb, f32[32,128]{1,0:T(8,128)S(1)} %get-tuple-element.11.ortho), custom_call_target="tpu_custom_call" | custom-call | tf_op jit(solution)/shard_map/apply/pallas_call | solution.py:335

commit v4 on v3

--- a/solution.py
+++ b/solution.py
@@ -13,6 +13,7 @@
 HALF, MPARTS = D // 2, 4
 NY, NX, NZ = 4, 4, 8
 WIDTH = 1024
+WAITS = sorted(((i, j) for i in range(4) for j in range(4) if i or j), key=lambda d: (min(d[0], 4 - d[0]) + min(d[1], 4 - d[1]), d))
 
 
 def pieces(value):
@@ -46,8 +47,8 @@
 
 def reduce_kernel(
     grad_hbm, error_hbm, basis_hbm, overflow, nb, ortho, ge,
-    bt, hb, mo, mi, mc, ly, gx, gz, t1, r1, t2, r2, zb,
-    in_sem, m_r, ly_r, gx_r, gz_r, p1_r, p2_r, z_r, a2_r, a1_r, ac_r, s_sem,
+    bt, hb, hs, mo, mi, mc, ly, gx, gz, t1, r1, t2, r2, zb,
+    in_sem, m_r, ly_r, hs_r, gx_r, gz_r, p1_r, p2_r, z_r, a_r, ac_r, s_sem,
 ):
     rep, shard = lax.axis_index("rep"), lax.axis_index("shard")
     y, c = rep // 2, rep % 2
@@ -58,11 +59,11 @@
 
     partner = at(y, 1 - c, x, z)
 
-    def along_y(d):
-        return at((y + d) % NY, c, x, z)
-
-    def along_x(d):
-        return at(y, c, (x + d) % NX, z)
+    def across(dx, dy):
+        return at((y + dy) % NY, c, (x + dx) % NX, z)
+
+    def slot(dx, dy):
+        return (x + dx) % NX * NY + (y + dy) % NY
 
     def along_z(d):
         return at(y, c, x, (z + d) % NZ)
@@ -82,7 +83,7 @@
         remote(like, like, s_sem.at[phase], m_r.at[0], partner).wait_send()
 
     def blocks(count):
-        return nb.at[pl.ds(0, count)]
+        return t1.at[pl.ds(0, count)]
 
     halves = [(1 - c) * HALF, c * HALF]
     loads = []
@@ -100,7 +101,8 @@
     barrier = pltpu.get_barrier_semaphore()
     replicas = [(2, 0), (2, 1), (1, 0), (3, 0), (1, 1), (3, 1), (0, 1)]
     replicas = [at((y + dy) % NY, (c + dc) % 2, x, z) for dy, dc in replicas]
-    others = replicas + [along_x(d) for d in range(1, NX)] + [along_z(d) for d in range(1, NZ)]
+    plane = [(dx, dy) for dx in (2, 1, 3, 0) for dy in (2, 1, 3, 0)]
+    others = replicas + [across(dx, dy) for dx, dy in plane if dx] + [along_z(d) for d in range(1, NZ)]
     for other in others:
         pl.semaphore_signal(barrier, inc=1, device_id=other, device_id_type=MESH)
 
@@ -152,34 +154,14 @@
             mc[rows, cols] = high
             mc[pl.ds(ROWS + k * size, size), cols] = (value - high.astype(F32)).astype(BF16)
     arrived(hb.at[1], m_r.at[MPARTS])
-    count = hb[0] + hb[1]
+    hs[y] = hb[0] + hb[1]
+    for d in (2, 1, 3):
+        send(hs.at[y], hs.at[y], 6, hs_r.at[0], across(0, d))
 
     arrived(ly.at[pl.ds(0, 7)], ly_r.at[0])
     left = ly[0]
     for i in range(1, 8):
         left = left + ly[i]
-
-    weighted = jnp.concatenate(pieces(left), axis=0)
-    weighted = jnp.concatenate([weighted, weighted], axis=1)
-    first = (x, y)
-    second = (y, x)
-    along_first = (along_x, along_y)
-    along_second = (along_y, along_x)
-    for d in (2, 1, 3, 0):
-        for h in range(2):
-            p = (first[h] + d) % 4
-            group = h * 16 + p * 4
-            cols = pl.ds(pl.multiple_of(group * 128, 512), 512)
-            out = lax.dot_general(weighted, mc[:, cols], (((1,), (0,)), ((), ())), preferred_element_type=F32)
-            value = out[:RANK] + out[RANK : 2 * RANK] + out[2 * RANK :]
-            for q in range(4):
-                part = value[:, q * 128 : (q + 1) * 128]
-                if d == 0:
-                    r1[h, p, q] = part
-                else:
-                    t1[group + q] = part
-            if d:
-                send(t1.at[pl.ds(group, 4)], r1.at[h, first[h]], 3, p1_r.at[h], along_first[h](d))
 
     gram = full_dot(left, jnp.concatenate([left] * 4, axis=0), ((1,), (1,)))
     lane_group = lax.broadcasted_iota(jnp.int32, (8, 128), 1) // RANK
@@ -188,7 +170,31 @@
         packed = jnp.where(lane_group == b, gram[8 * b : 8 * b + 8], packed)
     gx[x] = packed
     for d in (2, 1, 3):
-        send(gx.at[x], gx.at[x], 4, gx_r.at[0], along_x(d))
+        send(gx.at[x], gx.at[x], 4, gx_r.at[0], across(d, 0))
+    weighted = jnp.concatenate(pieces(left), axis=0)
+    weighted = jnp.concatenate([weighted, weighted], axis=1)
+    first = (x, y)
+    second = (y, x)
+    for d in (2, 1, 3, 0):
+        for h in range(2):
+            p = (first[h] + d) % 4
+            group = [h * 16 + (p * 4 + q, q * 4 + p)[h] for q in range(4)]
+            if h:
+                rows = jnp.concatenate([mc[:, pl.ds(pl.multiple_of(b * 128, 128), 128)] for b in group], axis=1)
+            else:
+                rows = mc[:, pl.ds(pl.multiple_of(group[0] * 128, 512), 512)]
+            out = lax.dot_general(weighted, rows, (((1,), (0,)), ((), ())), preferred_element_type=F32)
+            value = out[:RANK] + out[RANK : 2 * RANK] + out[2 * RANK :]
+            for q in range(4):
+                part = value[:, q * 128 : (q + 1) * 128]
+                if d == 0:
+                    r1[h, p, q] = part
+                else:
+                    t1[h * 16 + p * 4 + q] = part
+            if d:
+                target = across(0, d) if h else across(d, 0)
+                send(t1.at[pl.ds(h * 16 + p * 4, 4)], r1.at[h, first[h]], 3, p1_r.at[h], target)
+
     all_sent(hb.at[0], 0)
     all_sent(mo, 1)
     all_sent(blocks(7), 2)
@@ -200,21 +206,22 @@
     for h in range(2):
         arrived(blocks(12), p1_r.at[h])
         for q in range(4):
-            t2[h * 4 + q, :RANK] = r1[h, 0, q] + r1[h, 1, q] + r1[h, 2, q] + r1[h, 3, q]
-            t2[h * 4 + q, RANK:] = count
+            t2[h * 4 + q] = r1[h, 0, q] + r1[h, 1, q] + r1[h, 2, q] + r1[h, 3, q]
         for d in (2, 1, 3):
             q = (second[h] + d) % 4
-            send(t2.at[h * 4 + q], r2.at[h * 4 + second[h]], 6, p2_r.at[h], along_second[h](d))
+            target = across(d, 0) if h else across(0, d)
+            send(t2.at[h * 4 + q], r2.at[h * 4 + second[h]], 10, p2_r.at[h], target)
         r2[h * 4 + second[h]] = t2[h * 4 + second[h]]
     for h in range(2):
-        arrived(r2.at[pl.ds(0, 3)], p2_r.at[h])
-    for h in range(2):
-        zb[z, h] = r2[h * 4, :RANK] + r2[h * 4 + 1, :RANK] + r2[h * 4 + 2, :RANK] + r2[h * 4 + 3, :RANK]
-    for d in (4, 3, 5, 2, 6, 1, 7):
-        send(zb.at[z], zb.at[z], 7, z_r.at[0], along_z(d))
-    kept = r2[0, RANK:] + r2[1, RANK:] + r2[2, RANK:] + r2[3, RANK:]
+        arrived(blocks(3), p2_r.at[h])
+        zb[h, z] = r2[h * 4] + r2[h * 4 + 1] + r2[h * 4 + 2] + r2[h * 4 + 3]
+        for d in (4, 3, 5, 2, 6, 1, 7):
+            send(zb.at[h, z], zb.at[h, z], 7, z_r.at[h], along_z(d))
+    arrived(hs.at[pl.ds(0, 3)], hs_r.at[0])
+    kept = hs[0] + hs[1] + hs[2] + hs[3]
 
     all_sent(blocks(24), 3)
+    all_sent(blocks(6), 10)
     all_sent(gx.at[pl.ds(0, 3)], 4)
     all_sent(gz.at[pl.ds(0, 7)], 5)
     arrived(gz.at[pl.ds(0, 7)], gz_r.at[0])
@@ -223,36 +230,30 @@
         packed = packed + gz[i]
     gram = jnp.concatenate([packed] + [pltpu.roll(packed, 128 - RANK * b, 1) for b in range(1, 4)], axis=0)
     inverse = inverse_factor(gram)[:, :RANK]
+
+    me = slot(0, 0)
+    for h in range(2):
+        arrived(blocks(7), z_r.at[h])
+        value = zb[h, 0]
+        for i in range(1, NZ):
+            value = value + zb[h, i]
+        nb[c, h, me] = full_dot(inverse, value, ((1,), (0,))) / kept[:1]
+        mine = nb.at[c, h, me]
+        for dx, dy in plane[:-1]:
+            send(mine, mine, 8, a_r.at[h, me], across(dx, dy))
+        send(mine, mine, 9, ac_r.at[0], partner)
     ortho[...] = full_dot(inverse, left, ((1,), (0,)))
-    all_sent(r2.at[pl.ds(0, 6)], 6)
-
-    arrived(zb.at[pl.ds(0, 7)], z_r.at[0])
-    base = c * 32
+    all_sent(hs.at[pl.ds(0, 3)], 6)
+    all_sent(blocks(14), 7)
     for h in range(2):
-        value = zb[0, h]
-        for i in range(1, NZ):
-            value = value + zb[i, h]
-        block = base + h * 16 + first[h] * 4 + second[h]
-        nb[block] = full_dot(inverse, value, ((1,), (0,))) / kept[:1]
-        for d in (2, 1, 3):
-            send(nb.at[block], nb.at[block], 8, a2_r.at[h], along_second[h](d))
-    for h in range(2):
-        arrived(blocks(3), a2_r.at[h])
-        rows = pl.ds(base + h * 16 + first[h] * 4, 4)
-        for d in (2, 1, 3):
-            send(nb.at[rows], nb.at[rows], 9, a1_r.at[h, first[h]], along_first[h](d))
-        send(nb.at[rows], nb.at[rows], 10, ac_r.at[0], partner)
-    all_sent(blocks(14), 7)
-    all_sent(blocks(6), 8)
-    for d in (1, 3, 2):
-        for h in range(2):
-            p = (first[h] + d) % 4
-            rows = pl.ds(base + h * 16 + p * 4, 4)
-            arrived(nb.at[rows], a1_r.at[h, p])
-            send(nb.at[rows], nb.at[rows], 10, ac_r.at[0], partner)
-    all_sent(blocks(24), 9)
-    arrived(blocks(32), ac_r.at[0])
-    all_sent(blocks(32), 10)
+        for dx, dy in WAITS:
+            source = slot(dx, dy)
+            theirs = nb.at[c, h, source]
+            arrived(theirs, a_r.at[h, source])
+            send(theirs, theirs, 9, ac_r.at[0], partner)
+    all_sent(blocks(30), 8)
+    arrived(nb.at[1 - c], ac_r.at[0])
+    all_sent(blocks(32), 9)
 
 
 def apply_kernel(overflow, ge, nb, ortho, update_hbm, error_hbm, basis_hbm, update, new_error, basis, sem):
@@ -263,7 +264,7 @@
     for k in range(D // WIDTH):
         cols = pl.ds(k * WIDTH, WIDTH)
         count = WIDTH // 128
-        new_basis = jnp.concatenate([nb[k * count + i] for i in range(count)], axis=1)
+        new_basis = jnp.concatenate([nb[b // 32, b // 16 % 2, b % 16] for b in range(k * count, (k + 1) * count)], axis=1)
         basis[:, cols] = new_basis
         n1, n2, _ = pieces(new_basis)
         approx = lax.dot_general(
@@ -295,7 +296,7 @@
     nb, ortho, ge = pl.pallas_call(
         reduce_kernel,
         out_shape=[
-            vmem(64, *block),
+            vmem(2, 2, 16, *block),
             vmem(RANK, ROWS),
             pltpu.VMEM((2 * ROWS, D), BF16),
         ],
@@ -304,6 +305,7 @@
         scratch_shapes=[
             vmem(RANK, D),
             vmem(2, 8, 128),
+            vmem(NY, 8, 128),
             vmem(ROWS, HALF),
             vmem(ROWS, HALF),
             pltpu.VMEM((2 * ROWS, HALF), BF16),
@@ -312,19 +314,19 @@
             vmem(NZ, 8, 128),
             vmem(32, *block),
             vmem(2, 4, 4, *block),
-            vmem(8, RANK + 8, 128),
-            vmem(8, RANK + 8, 128),
-            vmem(NZ, 2, *block),
+            vmem(8, *block),
+            vmem(8, *block),
+            vmem(2, NZ, *block),
             dma((3, 2)),
             dma((MPARTS + 1,)),
             dma((1,)),
             dma((1,)),
             dma((1,)),
+            dma((1,)),
             dma((2,)),
             dma((2,)),
-            dma((1,)),
             dma((2,)),
-            dma((2, 4)),
+            dma((2, 16)),
             dma((1,)),
             dma((11,)),
         ],

time: 47 us -> 44.6 us (0.949)
  Pallas kernels: 45.7 us -> 43.2 us
    pallas_call x1, Pallas kernels: 42.9 us -> 40.4 us  [on_device(): pl.pallas_call(reduce_kernel, out_shape=[vmem(2, 2, 16, *block), vmem(RAN...]
where the time goes in v4:
time: 44.6 us; the launch traced here: 44.5 us
  Pallas kernels  43.2 us (97%)
  between operations  1.29 us (3%)
    pallas_call x1, Pallas kernels, on_device(): pl.pallas_call(reduce_kernel, out_shape=[vmem(2, 2, 16, *block), vmem(RAN...  40.4 us
    pallas_call x1, Pallas kernels, on_device(): pl.pallas_call(apply_kernel, out_shape=[jax.ShapeDtypeStruct((ROWS, D), B...  2.82 us

profile of v4, /device:TPU:1, one launch (start us, length us, event | category | flops | bytes accessed | tf_op | source)
XLA Modules:
  0.0 44.5 jit_solution(1841508347887685946)
XLA Ops:
  1.3 40.4 %reduce.1 = (f32[2,2,16,32,128]{4,3,2,1,0:T(8,128)S(1)}, f32[32,128]{1,0:T(8,128)S(1)}, bf16[256,8192]{1,0:T(8,128)(2,1)S(1)}) custom-call(bf16[128,8192]{1,0:T(8,128)(2,1)} %bitcast.5, bf16[128,8192]{1,0:T(8,128)(2,1)} %bitcast.6, f32[32,8192]{1,0:T(8,128)} %bitcast.7, s32[1]{0:T(128)S(6)} %copy.7.overflow), custom_call_target="tpu_custom_call" | custom-call | tf_op jit(solution)/shard_map/reduce/pallas_call | solution.py:296
  41.7 2.8 %apply.1 = (bf16[128,8192]{1,0:T(8,128)(2,1)}, bf16[128,8192]{1,0:T(8,128)(2,1)}, f32[32,8192]{1,0:T(8,128)}) custom-call(s32[1]{0:T(128)S(6)} %copy.7.overflow, bf16[256,8192]{1,0:T(8,128)(2,1)S(1)} %get-tuple-element.9.ge, f32[2,2,16,32,128]{4,3,2,1,0:T(8,128)S(1)} %get-tuple-element.10.nb, f32[32,128]{1,0:T(8,128)S(1)} %get-tuple-element.11.ortho), custom_call_target="tpu_custom_call" | custom-call | tf_op jit(solution)/shard_map/apply/pallas_call | solution.py:337

commit v5 on v4

--- a/solution.py
+++ b/solution.py
@@ -10,7 +10,7 @@
 MESH = pl.DeviceIdType.MESH
 F32, BF16 = jnp.float32, jnp.bfloat16
 D, RANK, ROWS = 8192, 32, 128
-HALF, MPARTS = D // 2, 4
+HALF, QUARTER, MPARTS = D // 2, D // 4, 4
 NY, NX, NZ = 4, 4, 8
 WIDTH = 1024
 WAITS = sorted(((i, j) for i in range(4) for j in range(4) if i or j), key=lambda d: (min(d[0], 4 - d[0]) + min(d[1], 4 - d[1]), d))
@@ -46,7 +46,7 @@
 
 
 def reduce_kernel(
-    grad_hbm, error_hbm, basis_hbm, overflow, nb, ortho, ge,
+    grad_hbm, error_hbm, basis_hbm, overflow, nb, ortho, ge, update, new_error, new_basis,
     bt, hb, hs, mo, mi, mc, ly, gx, gz, t1, r1, t2, r2, zb,
     in_sem, m_r, ly_r, hs_r, gx_r, gz_r, p1_r, p2_r, z_r, a_r, ac_r, s_sem,
 ):
@@ -215,7 +215,7 @@
     for h in range(2):
         arrived(blocks(3), p2_r.at[h])
         zb[h, z] = r2[h * 4] + r2[h * 4 + 1] + r2[h * 4 + 2] + r2[h * 4 + 3]
-        for d in (4, 3, 5, 2, 6, 1, 7):
+        for d in (1, 7, 2, 6, 3, 5, 4):
             send(zb.at[h, z], zb.at[h, z], 7, z_r.at[h], along_z(d))
     arrived(hs.at[pl.ds(0, 3)], hs_r.at[0])
     kept = hs[0] + hs[1] + hs[2] + hs[3]
@@ -241,46 +241,71 @@
         mine = nb.at[c, h, me]
         for dx, dy in plane[:-1]:
             send(mine, mine, 8, a_r.at[h, me], across(dx, dy))
-        send(mine, mine, 9, ac_r.at[0], partner)
+        send(mine, mine, 9, ac_r.at[h], partner)
     ortho[...] = full_dot(inverse, left, ((1,), (0,)))
     all_sent(hs.at[pl.ds(0, 3)], 6)
     all_sent(blocks(14), 7)
+    left_pieces = stacked(ortho[...])
+
+    def finish(core, h):
+        for k in range(QUARTER // WIDTH):
+            cols = pl.ds(pl.multiple_of(core * HALF + h * QUARTER + k * WIDTH, WIDTH), WIDTH)
+            values = [nb[core, h, k * (WIDTH // 128) + i] for i in range(WIDTH // 128)]
+            apply(health[:1, :1], left_pieces, values, ge, update, new_error, new_basis, cols, cols)
+
     for h in range(2):
         for dx, dy in WAITS:
             source = slot(dx, dy)
             theirs = nb.at[c, h, source]
             arrived(theirs, a_r.at[h, source])
-            send(theirs, theirs, 9, ac_r.at[0], partner)
+            send(theirs, theirs, 9, ac_r.at[h], partner)
+        finish(c, h)
     all_sent(blocks(30), 8)
-    arrived(nb.at[1 - c], ac_r.at[0])
+    arrived(blocks(16), ac_r.at[0])
+    finish(1 - c, 0)
+    arrived(blocks(16), ac_r.at[1])
     all_sent(blocks(32), 9)
 
 
-def apply_kernel(overflow, ge, nb, ortho, update_hbm, error_hbm, basis_hbm, update, new_error, basis, sem):
+def stacked(ortho):
+    o1, o2, _ = pieces(ortho)
+    return jnp.concatenate([o1, o1, o2], axis=0)
+
+
+def apply(health, ortho_pieces, blocks, ge, update, new_error, basis, cols, to):
+    value = jnp.concatenate(blocks, axis=1)
+    basis[:, to] = value
+    n1, n2, _ = pieces(value)
+    approx = lax.dot_general(
+        ortho_pieces, jnp.concatenate([n1, n2, n1], axis=0), (((0,), (0,)), ((), ())), preferred_element_type=F32
+    )
+    update[:, to] = approx.astype(BF16)
+    error_value = ge[ROWS:, cols].astype(F32)
+    corrected = ge[:ROWS, cols].astype(F32) + error_value
+    new_error[:, to] = jnp.where(health > 0.5, corrected - approx, error_value).astype(BF16)
+
+
+def last_kernel(
+    overflow, nb, ortho, ge, update, new_error, basis, update_hbm, error_hbm, basis_hbm, update_s, error_s, basis_s, sem
+):
+    c = lax.axis_index("rep") % 2
+    results = ((update, update_s, update_hbm), (new_error, error_s, error_hbm), (basis, basis_s, basis_hbm))
+    copies = []
+    for k, start in enumerate((c * HALF, c * HALF + QUARTER, (1 - c) * HALF)):
+        cols = pl.ds(pl.multiple_of(start, QUARTER), QUARTER)
+        for i, (done, _, out) in enumerate(results):
+            copies.append(pltpu.make_async_copy(done.at[:, cols], out.at[:, cols], sem.at[i, k]))
+            copies[-1].start()
     health = 1.0 - overflow[0].astype(F32)
-    o1, o2, _ = pieces(ortho[...])
-    ortho_pieces = jnp.concatenate([o1, o1, o2], axis=0)
-    copies = []
-    for k in range(D // WIDTH):
-        cols = pl.ds(k * WIDTH, WIDTH)
-        count = WIDTH // 128
-        new_basis = jnp.concatenate([nb[b // 32, b // 16 % 2, b % 16] for b in range(k * count, (k + 1) * count)], axis=1)
-        basis[:, cols] = new_basis
-        n1, n2, _ = pieces(new_basis)
-        approx = lax.dot_general(
-            ortho_pieces,
-            jnp.concatenate([n1, n2, n1], axis=0),
-            (((0,), (0,)), ((), ())),
-            preferred_element_type=F32,
-        )
-        update[:, cols] = approx.astype(BF16)
-        error_value = ge[ROWS:, cols].astype(F32)
-        corrected = ge[:ROWS, cols].astype(F32) + error_value
-        new_error[:, cols] = jnp.where(health > 0.5, corrected - approx, error_value).astype(BF16)
-        for i, (value, out) in enumerate(((basis, basis_hbm), (update, update_hbm), (new_error, error_hbm))):
-            copy = pltpu.make_async_copy(value.at[:, cols], out.at[:, cols], sem.at[i, k])
-            copy.start()
-            copies.append(copy)
+    ortho_pieces = stacked(ortho[...])
+    for k in range(QUARTER // WIDTH):
+        to = pl.ds(k * WIDTH, WIDTH)
+        cols = pl.ds(pl.multiple_of((1 - c) * HALF + QUARTER + k * WIDTH, WIDTH), WIDTH)
+        values = [nb[1 - c, 1, k * (WIDTH // 128) + i] for i in range(WIDTH // 128)]
+        apply(health, ortho_pieces, values, ge, update_s, error_s, basis_s, cols, to)
+        for i, (_, new, out) in enumerate(results):
+            copies.append(pltpu.make_async_copy(new.at[:, to], out.at[:, cols], sem.at[i, 3 + k]))
+            copies[-1].start()
     for copy in copies:
         copy.wait()
 
@@ -293,15 +318,18 @@
     vmem = lambda *shape: pltpu.VMEM(shape, F32)
     block = (RANK, 128)
     operands = [pltpu.with_memory_space_constraint(a, pltpu.HBM) for a in (grad, error, basis_out.T)]
-    nb, ortho, ge = pl.pallas_call(
+    outs = pl.pallas_call(
         reduce_kernel,
         out_shape=[
             vmem(2, 2, 16, *block),
             vmem(RANK, ROWS),
             pltpu.VMEM((2 * ROWS, D), BF16),
+            pltpu.VMEM((ROWS, D), BF16),
+            pltpu.VMEM((ROWS, D), BF16),
+            vmem(RANK, D),
         ],
         in_specs=[hbm, hbm, hbm, smem],
-        out_specs=[whole, whole, whole],
+        out_specs=[whole] * 6,
         scratch_shapes=[
             vmem(RANK, D),
             vmem(2, 8, 128),
@@ -327,7 +355,7 @@
             dma((2,)),
             dma((2,)),
             dma((2, 16)),
-            dma((1,)),
+            dma((2,)),
             dma((11,)),
         ],
         compiler_params=pltpu.CompilerParams(collective_id=0, has_side_effects=True, vmem_limit_bytes=32 << 20),
@@ -335,20 +363,20 @@
     )(*operands, overflow)
 
     update, new_error, new_basis = pl.pallas_call(
-        apply_kernel,
+        last_kernel,
         out_shape=[
             jax.ShapeDtypeStruct((ROWS, D), BF16),
             jax.ShapeDtypeStruct((ROWS, D), BF16),
             jax.ShapeDtypeStruct((RANK, D), F32),
         ],
-        in_specs=[smem, whole, whole, whole],
+        in_specs=[smem] + [whole] * 6,
         out_specs=[hbm, hbm, hbm],
         scratch_shapes=[
-            pltpu.VMEM((ROWS, D), BF16), pltpu.VMEM((ROWS, D), BF16), vmem(RANK, D), dma((3, D // WIDTH))
+            pltpu.VMEM((ROWS, QUARTER), BF16), pltpu.VMEM((ROWS, QUARTER), BF16), vmem(RANK, QUARTER), dma((3, 3 + QUARTER // WIDTH))
         ],
-        compiler_params=pltpu.CompilerParams(vmem_limit_bytes=24 << 20),
-        name="apply",
-    )(overflow, ge, nb, ortho)
+        compiler_params=pltpu.CompilerParams(vmem_limit_bytes=16 << 20),
+        name="last",
+    )(overflow, *outs)
     return update, new_error[None], new_basis.T
 
 

time: 44.6 us -> 44.3 us (level)
  no operation moved by 1% of the time
where the time goes in v5:
time: 44.3 us; the launch traced here: 44.2 us
  Pallas kernels  42.9 us (97%)
  between operations  1.29 us (3%)
    pallas_call x1, Pallas kernels, on_device(): pl.pallas_call(reduce_kernel, out_shape=[vmem(2, 2, 16, *block), vmem(RAN...  40.4 us
    pallas_call x1, Pallas kernels, on_device(): pl.pallas_call(last_kernel, out_shape=[jax.ShapeDtypeStruct((ROWS, D), BF...  2.56 us

profile of v5, /device:TPU:1, one launch (start us, length us, event | category | flops | bytes accessed | tf_op | source)
XLA Modules:
  0.0 44.2 jit_solution(4767445650945749081)
XLA Ops:
  1.3 40.4 %reduce.1 = (f32[2,2,16,32,128]{4,3,2,1,0:T(8,128)S(1)}, f32[32,128]{1,0:T(8,128)S(1)}, bf16[256,8192]{1,0:T(8,128)(2,1)S(1)}, bf16[128,8192]{1,0:T(8,128)(2,1)S...) custom-call(bf16[128,8192]{1,0:T(8,128)(2,1)} %bitcast.5, bf16[128,8192]{1,0:T(8,128)(2,1)} %bitcast.6, ...), custom_call_target="tpu_custom_call" | custom-call | tf_op jit(solution)/shard_map/reduce/pallas_call | solution.py:321
  41.7 2.6 %last.1 = (bf16[128,8192]{1,0:T(8,128)(2,1)}, bf16[128,8192]{1,0:T(8,128)(2,1)}, f32[32,8192]{1,0:T(8,128)}) custom-call(s32[1]{0:T(128)S(6)} %copy.7.overflow, f32[2,2,16,32,128]{4,3,2,1,0:T(8,128)S(1)} %get-tuple-element.12.nb, f32[32,128]{1,0:T(8,128)S(1)} %get-tuple-element.13.ortho, bf16[256,8192]{1,0:T(8,128)(2,1)S(1)} %get-tuple-element.14.ge, ...), custom_call_target="tpu_custom_call" | custom-call | tf_op jit(solution)/shard_map/last/pallas_call | solution.py:365

commit v6 on v5

--- a/solution.py
+++ b/solution.py
@@ -10,7 +10,7 @@
 MESH = pl.DeviceIdType.MESH
 F32, BF16 = jnp.float32, jnp.bfloat16
 D, RANK, ROWS = 8192, 32, 128
-HALF, QUARTER, MPARTS = D // 2, D // 4, 4
+HALF, QUARTER, MPARTS = D // 2, D // 4, 2
 NY, NX, NZ = 4, 4, 8
 WIDTH = 1024
 WAITS = sorted(((i, j) for i in range(4) for j in range(4) if i or j), key=lambda d: (min(d[0], 4 - d[0]) + min(d[1], 4 - d[1]), d))
@@ -99,7 +99,7 @@
         loads.append(group)
 
     barrier = pltpu.get_barrier_semaphore()
-    replicas = [(2, 0), (2, 1), (1, 0), (3, 0), (1, 1), (3, 1), (0, 1)]
+    replicas = [(2, 1), (1, 1), (3, 1), (2, 0), (1, 0), (3, 0), (0, 1)]
     replicas = [at((y + dy) % NY, (c + dc) % 2, x, z) for dy, dc in replicas]
     plane = [(dx, dy) for dx in (2, 1, 3, 0) for dy in (2, 1, 3, 0)]
     others = replicas + [across(dx, dy) for dx, dy in plane if dx] + [along_z(d) for d in range(1, NZ)]
@@ -215,7 +215,7 @@
     for h in range(2):
         arrived(blocks(3), p2_r.at[h])
         zb[h, z] = r2[h * 4] + r2[h * 4 + 1] + r2[h * 4 + 2] + r2[h * 4 + 3]
-        for d in (1, 7, 2, 6, 3, 5, 4):
+        for d in (4, 3, 5, 2, 6, 1, 7):
             send(zb.at[h, z], zb.at[h, z], 7, z_r.at[h], along_z(d))
     arrived(hs.at[pl.ds(0, 3)], hs_r.at[0])
     kept = hs[0] + hs[1] + hs[2] + hs[3]

time: 44.3 us -> 43.6 us (0.984)
  Pallas kernels: 42.9 us -> 42.3 us
    pallas_call x1, Pallas kernels: 40.4 us -> 39.7 us  [on_device(): pl.pallas_call(reduce_kernel, out_shape=[vmem(2, 2, 16, *block), vmem(RAN...]
where the time goes in v6:
time: 43.6 us; the launch traced here: 43.5 us
  Pallas kernels  42.3 us (97%)
  between operations  1.29 us (3%)
    pallas_call x1, Pallas kernels, on_device(): pl.pallas_call(reduce_kernel, out_shape=[vmem(2, 2, 16, *block), vmem(RAN...  39.7 us
    pallas_call x1, Pallas kernels, on_device(): pl.pallas_call(last_kernel, out_shape=[jax.ShapeDtypeStruct((ROWS, D), BF...  2.56 us

profile of v6, /device:TPU:1, one launch (start us, length us, event | category | flops | bytes accessed | tf_op | source)
XLA Modules:
  0.0 43.5 jit_solution(10607273044743065708)
XLA Ops:
  1.3 39.7 %reduce.1 = (f32[2,2,16,32,128]{4,3,2,1,0:T(8,128)S(1)}, f32[32,128]{1,0:T(8,128)S(1)}, bf16[256,8192]{1,0:T(8,128)(2,1)S(1)}, bf16[128,8192]{1,0:T(8,128)(2,1)S...) custom-call(bf16[128,8192]{1,0:T(8,128)(2,1)} %bitcast.5, bf16[128,8192]{1,0:T(8,128)(2,1)} %bitcast.6, ...), custom_call_target="tpu_custom_call" | custom-call | tf_op jit(solution)/shard_map/reduce/pallas_call | solution.py:321
  41.0 2.6 %last.1 = (bf16[128,8192]{1,0:T(8,128)(2,1)}, bf16[128,8192]{1,0:T(8,128)(2,1)}, f32[32,8192]{1,0:T(8,128)}) custom-call(s32[1]{0:T(128)S(6)} %copy.7.overflow, f32[2,2,16,32,128]{4,3,2,1,0:T(8,128)S(1)} %get-tuple-element.12.nb, f32[32,128]{1,0:T(8,128)S(1)} %get-tuple-element.13.ortho, bf16[256,8192]{1,0:T(8,128)(2,1)S(1)} %get-tuple-element.14.ge, ...), custom_call_target="tpu_custom_call" | custom-call | tf_op jit(solution)/shard_map/last/pallas_call | solution.py:365

commit v7 on v6

--- a/solution.py
+++ b/solution.py
@@ -195,9 +195,6 @@
                 target = across(0, d) if h else across(d, 0)
                 send(t1.at[pl.ds(h * 16 + p * 4, 4)], r1.at[h, first[h]], 3, p1_r.at[h], target)
 
-    all_sent(hb.at[0], 0)
-    all_sent(mo, 1)
-    all_sent(blocks(7), 2)
     arrived(gx.at[pl.ds(0, 3)], gx_r.at[0])
     gz[z] = gx[0] + gx[1] + gx[2] + gx[3]
     for d in (4, 3, 5, 2, 6, 1, 7):
@@ -220,10 +217,6 @@
     arrived(hs.at[pl.ds(0, 3)], hs_r.at[0])
     kept = hs[0] + hs[1] + hs[2] + hs[3]
 
-    all_sent(blocks(24), 3)
-    all_sent(blocks(6), 10)
-    all_sent(gx.at[pl.ds(0, 3)], 4)
-    all_sent(gz.at[pl.ds(0, 7)], 5)
     arrived(gz.at[pl.ds(0, 7)], gz_r.at[0])
     packed = gz[0]
     for i in range(1, NZ):
@@ -243,6 +236,13 @@
             send(mine, mine, 8, a_r.at[h, me], across(dx, dy))
         send(mine, mine, 9, ac_r.at[h], partner)
     ortho[...] = full_dot(inverse, left, ((1,), (0,)))
+    all_sent(hb.at[0], 0)
+    all_sent(mo, 1)
+    all_sent(blocks(7), 2)
+    all_sent(blocks(24), 3)
+    all_sent(blocks(6), 10)
+    all_sent(gx.at[pl.ds(0, 3)], 4)
+    all_sent(gz.at[pl.ds(0, 7)], 5)
     all_sent(hs.at[pl.ds(0, 3)], 6)
     all_sent(blocks(14), 7)
     left_pieces = stacked(ortho[...])
@@ -260,10 +260,10 @@
             arrived(theirs, a_r.at[h, source])
             send(theirs, theirs, 9, ac_r.at[h], partner)
         finish(c, h)
-    all_sent(blocks(30), 8)
     arrived(blocks(16), ac_r.at[0])
     finish(1 - c, 0)
     arrived(blocks(16), ac_r.at[1])
+    all_sent(blocks(30), 8)
     all_sent(blocks(32), 9)
 
 

time: 43.6 us -> 43.6 us (level)
  no operation moved by 1% of the time
where the time goes in v7:
time: 43.6 us
  Pallas kernels  42.3 us (97%)
  between operations  1.29 us (3%)
    pallas_call x1, Pallas kernels, on_device(): pl.pallas_call(reduce_kernel, out_shape=[vmem(2, 2, 16, *block), vmem(RAN...  39.7 us
    pallas_call x1, Pallas kernels, on_device(): pl.pallas_call(last_kernel, out_shape=[jax.ShapeDtypeStruct((ROWS, D), BF...  2.56 us

profile of v7, /device:TPU:1, one launch (start us, length us, event | category | flops | bytes accessed | tf_op | source)
XLA Modules:
  0.0 43.6 jit_solution(13317606832801806301)
XLA Ops:
  1.3 39.7 %reduce.1 = (f32[2,2,16,32,128]{4,3,2,1,0:T(8,128)S(1)}, f32[32,128]{1,0:T(8,128)S(1)}, bf16[256,8192]{1,0:T(8,128)(2,1)S(1)}, bf16[128,8192]{1,0:T(8,128)(2,1)S...) custom-call(bf16[128,8192]{1,0:T(8,128)(2,1)} %bitcast.5, bf16[128,8192]{1,0:T(8,128)(2,1)} %bitcast.6, ...), custom_call_target="tpu_custom_call" | custom-call | tf_op jit(solution)/shard_map/reduce/pallas_call | solution.py:321
  41.0 2.6 %last.1 = (bf16[128,8192]{1,0:T(8,128)(2,1)}, bf16[128,8192]{1,0:T(8,128)(2,1)}, f32[32,8192]{1,0:T(8,128)}) custom-call(s32[1]{0:T(128)S(6)} %copy.7.overflow, f32[2,2,16,32,128]{4,3,2,1,0:T(8,128)S(1)} %get-tuple-element.12.nb, f32[32,128]{1,0:T(8,128)S(1)} %get-tuple-element.13.ortho, bf16[256,8192]{1,0:T(8,128)(2,1)S(1)} %get-tuple-element.14.ge, ...), custom_call_target="tpu_custom_call" | custom-call | tf_op jit(solution)/shard_map/last/pallas_call | solution.py:365
